TPU v7x, 512 devices: a whole 4x8x8 slice. The times are simulated.
512 devices in a mesh: dp: 64 (over z, x, core), tensor: 8 (over y).
Axes of the slice: x: 4, y: 8, z: 8, core: 2. Of those that a mesh axis runs over, the one named last changes fastest.
Arguments:
- acts: bfloat16 [16384, 8192], P('dp', 'tensor'), may hold values from -6 to 6
- mean_vec: float32 [8192], P('tensor'), may hold values from -3 to 3
- left_factor: bfloat16 [512, 8192], P('dp', 'tensor'), may hold values from -0.25 to 0.25
- right_factor: bfloat16 [512, 8192], P('dp', 'tensor'), may hold values from -0.0625 to 0.0625
- labels: int32 [16384], P('dp'), may hold values from 0 to 511, as said below
- counts: int32 [64], P('dp'), may hold values from 69 to 256, as said below
Outputs:
- erased: bfloat16 [16384, 8192], P('dp', 'tensor')
- class_scores: float32 [512, 8192], P('dp', 'tensor')
- class_counts: int32 [512], P('dp')
Inputs may be any that keep to these rules, and one draw needn't show every extreme that they name: `counts`: some data shard is full. `labels`: class frequencies are skewed; at least two classes occur in no token slot.
All inputs are finite; a program needn't handle non-finite values.
Results may differ from a plain program's by a relative error of at most 0.0053.
Values may be sent and summed in bfloat16 or wider, within the bound.
A program may use at most 64 MiB of HBM per device.

v0:
```python
import jax
import jax.numpy as jnp
from jax import lax
from jax.sharding import PartitionSpec as P

C = 512


def per_device(acts, mean_vec, left_factor, right_factor, labels, counts):
    row_count = acts.shape[0]
    centred = (acts.astype(jnp.float32) - mean_vec[None, :]).astype(jnp.bfloat16)
    right_full, left_full = (
        lax.all_gather(right_factor, "dp", axis=0, tiled=True),
        lax.all_gather(left_factor, "dp", axis=0, tiled=True),
    )
    coord_part = lax.dot_general(
        centred, right_full, (((1,), (1,)), ((), ())), preferred_element_type=jnp.float32
    )
    coords = lax.psum(coord_part, "tensor").astype(jnp.bfloat16)
    correction = jnp.dot(coords, left_full, preferred_element_type=jnp.float32)
    erased = (acts.astype(jnp.float32) - correction).astype(jnp.bfloat16)
    valid_rows = jnp.arange(row_count, dtype=jnp.int32) < counts[0]
    label_hits = (labels[:, None] == jnp.arange(C, dtype=jnp.int32)[None, :]) & valid_rows[:, None]
    onehot = label_hits.astype(jnp.bfloat16)
    count_part = jnp.sum(label_hits.astype(jnp.float32), axis=0)
    feature_part = jnp.dot(
        valid_rows.astype(jnp.bfloat16), erased, preferred_element_type=jnp.float32
    )
    counts_all, totals_all = lax.psum((count_part, feature_part), "dp")
    grand_total = jnp.sum(counts_all)
    feature_mean = totals_all / grand_total
    own_classes = C // lax.axis_size("dp")
    first_class = lax.axis_index("dp") * own_classes
    own_counts = lax.dynamic_slice_in_dim(counts_all, first_class, own_classes, 0)
    class_sums = lax.psum_scatter(
        lax.dot_general(
            onehot, erased, (((0,), (0,)), ((), ())), preferred_element_type=jnp.float32
        ),
        "dp",
        scatter_dimension=0,
        tiled=True,
    )
    deviations = class_sums - own_counts[:, None] * feature_mean[None, :]
    scale_rows = 1.0 / jnp.sqrt(jnp.maximum(own_counts, 1.0))
    class_scores = deviations * scale_rows[:, None]
    return (erased, class_scores, own_counts.astype(jnp.int32))


def solution(mesh):
    return jax.shard_map(
        per_device,
        mesh=mesh,
        in_specs=(
            P("dp", "tensor"),
            P("tensor"),
            P("dp", "tensor"),
            P("dp", "tensor"),
            P("dp"),
            P("dp"),
        ),
        out_specs=(P("dp", "tensor"), P("dp", "tensor"), P("dp")),
        check_vma=False,
    )
```

profile of v0, /device:TPU:1, one launch (start us, length us, event | category | flops | bytes accessed | tf_op | source)
XLA Modules:
  0.0 391.1 jit_solution(10929585995187992876)
XLA Ops:
  7.2 0.0 copy-start.1
  7.2 0.0 all-gather.3.cloned.1.call-start
  7.2 0.7 all-gather.3.cloned.1.call-update
  7.9 0.0 all-gather.5.cloned.1.call-start
  8.0 0.7 all-gather.5.cloned.1.call-update
  8.7 0.0 all-reduce.5.cloned.1.call-start
  9.4 90.4 %all-gather.3.cloned.1.call-done = bf16[512,1024]{1,0:T(8,128)(2,1)} async-done(((bf16[8,1024]{1,0:T(8,128)(2,1)}), bf16[512,1024]{1,0:T(8,128)(2,1)}) %all-gather.3.cloned.1.call-update) | async-done | bytes 1048592 | tf_op jit(solution)/shard_map/all_gather | solution.py:13
  99.8 1.9 fusion.2
  101.6 0.0 copy-start.2
  101.7 30.1 %all-reduce.6 = bf16[256,512]{1,0:T(8,128)(2,1)S(1)} all-reduce(f32[256,512]{1,0:T(8,128)S(1)} %fusion.2), channel_id=1, replica_groups=mesh['dp'=64,'tensor'=8] {'tensor'}, use_global_device_ids=true, to_apply=%region_0.0 | all-reduce | flops 131072 | bytes 786432 | tf_op jit(solution)/shard_map/psum | solution.py:19
  131.8 51.1 %all-gather.5.cloned.1.call-done = bf16[512,1024]{1,0:T(8,128)(2,1)} async-done(((bf16[8,1024]{1,0:T(8,128)(2,1)}), bf16[512,1024]{1,0:T(8,128)(2,1)}) %all-gather.5.cloned.1.call-update) | async-done | bytes 1048592 | tf_op jit(solution)/shard_map/all_gather | solution.py:14
  182.9 0.0 copy-done.1
  182.9 1.7 fusion
  184.6 0.0 copy-done.2
  184.6 0.0 copy-start
  184.6 1.9 fusion.6
  186.5 0.0 all-reduce.5.cloned.1.call-update
  186.5 1.3 dynamic-slice
  188.4 0.2 convert_reduce_fusion
  188.6 0.0 copy-done
  188.6 0.2 fusion.13
  188.8 125.8 %all-reduce.1 = (f32[512]{0:T(512)S(1)}, f32[1024]{0:T(1024)S(1)}) all-reduce(f32[512]{0:T(512)S(1)} %convert_reduce_fusion, f32[1024]{0:T(1024)S(1)} %bitcast.10), channel_id=1, replica_groups=mesh['dp'=64,'tensor'=8] {'dp'}, use_global_device_ids=true, to_apply=%region_3.0 | all-reduce | flops 1536 | bytes 12288 | tf_op jit(solution)/shard_map/psum | solution.py:29
  314.6 0.6 reduce_sum.19
  315.2 0.6 fusion.12
  315.8 0.7 broadcast_divide_fusion
  316.4 66.7 %all-reduce.5.cloned.1.call-done = f32[512,1024]{1,0:T(8,128)} async-done(((f32[512,1024]{1,0:T(8,128)}), f32[512,1024]{1,0:T(8,128)}) %all-reduce.5.cloned.1.call-update) | async-done | bytes 2097168
  383.1 1.4 fusion.11
  (3 shorter events, 0.0 us)
Async XLA Ops:
  7.2 175.7 %copy-start.1 = (bf16[256,1024]{1,0:T(8,128)(2,1)S(1)}, bf16[256,1024]{1,0:T(8,128)(2,1)}, u32[]{:S(2)}) copy-start(bf16[256,1024]{1,0:T(8,128)(2,1)} %param.6) | copy-start | bytes 1572868
  7.2 92.6 %all-gather.3.cloned.1.call-start = ((), (), s32[]{:S(2)}) async-start(), calls=%async_computation | async-start | bytes 1064960 | tf_op jit(solution)/shard_map/all_gather | solution.py:13
  7.9 175.0 %all-gather.5.cloned.1.call-start = ((), (), s32[]{:S(2)}) async-start(), calls=%async_computation.1 | async-start | bytes 1064960 | tf_op jit(solution)/shard_map/all_gather | solution.py:14
  8.7 374.4 %all-reduce.5.cloned.1.call-start = ((), (), s32[]{:S(2)}) async-start(), calls=%async_computation.2 | async-start | bytes 4194304
  101.6 82.9 %copy-start.2 = (s32[256]{0:T(256)S(1)}, s32[256]{0:T(256)}, u32[]{:S(2)}) copy-start(s32[256]{0:T(256)} %param.10) | copy-start | bytes 3076
  184.6 4.0 %copy-start = (bf16[256,1024]{1,0:T(8,128)(2,1)}, bf16[256,1024]{1,0:T(8,128)(2,1)S(1)}, u32[]{:S(2)}) copy-start(bf16[256,1024]{1,0:T(8,128)(2,1)S(1)} %fusion) | copy-start | bytes 1572868
Sparse Core Ops, SparseCore 0:
  11.4 88.3 all-gather.2
  103.1 79.7 all-gather.4
  186.6 196.4 all-reduce.4
where the time goes:
time: 392 us; the launch traced here: 391 us
  waiting for transfers between devices  210 us (54%)
  blocking collectives  156 us (40%)
  between operations  15.2 us (4%)
  matrix products  5.59 us (1%)
    psum x1, blocking collectives, per_device(): counts_all, totals_all = lax.psum((count_part, feature_part), 'dp')  126 us
    all_gather x1, waiting for transfers between devices, per_device(): lax.all_gather(right_factor, 'dp', axis=0, tiled=True)  90.4 us
    unnamed x4, waiting for transfers between devices  68.1 us
    all_gather x1, waiting for transfers between devices, per_device(): lax.all_gather(left_factor, 'dp', axis=0, tiled=True)  51.1 us
    psum x1, blocking collectives, per_device(): coords = lax.psum(coord_part, 'tensor').astype(jnp.bfloat16)  30.1 us
  transfers between devices with their start and end apart: 3, of which 3 were waited for; matrix products, arithmetic and copies ran while one was open for 1% of the time, Pallas kernels for 0%

commit v1 on v0

v1 whole, which is shorter than its diff:
```python
import functools

import jax
import jax.numpy as jnp
from jax import lax
from jax.experimental import pallas as pl
from jax.experimental.pallas import tpu as pltpu
from jax.sharding import PartitionSpec as P

MESH = pl.DeviceIdType.MESH
F32, BF16 = jnp.float32, jnp.bfloat16
C = 512
NZ, NX, NY = 8, 4, 8
ZORD = (0, 1, 7, 2, 6, 3, 5, 4)
XORD = (0, 1, 3, 2)
ZPOS = {d: s for s, d in enumerate(ZORD)}
XPOS = {d: s for s, d in enumerate(XORD)}
FAR = (7, 6, 5, 4, 3, 2, 1)
GROUPS = ((0, 2), (2, 2), (4, 2), (6, 2))
TOK, D, RD = 256, 1024, 8
T2, H, K2 = 512, 512, 128
QN = 2
QW = H // QN
YB = T2 // NY


def kernel(
    acts, mean, left, right, labels, counts,
    out, scores, cnt,
    actv, cen, rg, lg, lm, lab, pbuf, prx, cbuf, oh, er,
    sxs, sxr, s0, txs, txr, szs, szr, tzs, tzr,
    loc, rzs, rzr, rxs, rxr, lzs, lzr, lxs, lxr, bzs, bzr, bxs, bxr, exs, exr,
    pss, psr, css, csr, xxs, xxr, zzs, zzr,
):
    dp, y = lax.axis_index("dp"), lax.axis_index("tensor")
    c, x, z = lax.rem(dp, 2), lax.rem(dp // 2, NX), dp // (2 * NX)
    oc = 1 - c

    def dev(dz=0, dx=0, core=None, dy=0):
        core = c if core is None else core
        zz, xx, yy = lax.rem(z + dz, NZ), lax.rem(x + dx, NX), lax.rem(y + dy, NY)
        return ((zz * NX + xx) * 2 + core, yy)

    sent = []

    def send(src, dst, ss, rs, to):
        cp = pltpu.make_async_remote_copy(
            src_ref=src, dst_ref=dst, send_sem=ss, recv_sem=rs, device_id=to, device_id_type=MESH
        )
        cp.start()
        sent.append(cp)

    def got(dst, rs):
        pltpu.make_async_remote_copy(
            src_ref=dst, dst_ref=dst, send_sem=rs, recv_sem=rs, device_id=dev(core=oc), device_id_type=MESH
        ).wait_recv()

    mine = pl.ds(pl.multiple_of(c * TOK, TOK), TOK)
    theirs = pl.ds(pl.multiple_of(oc * TOK, TOK), TOK)
    loads = [
        pltpu.make_async_copy(right, rg.at[0, 0], loc.at[0]),
        pltpu.make_async_copy(acts, actv.at[mine], loc.at[1]),
    ]
    for cp in loads:
        cp.start()

    barrier = pltpu.get_barrier_semaphore()
    peers = [dev(dz=d, core=k) for d in range(1, NZ) for k in (c, oc)]
    peers += [dev(dx=d) for d in range(1, NX)] + [dev(dy=d) for d in range(1, NY)] + [dev(core=oc)]
    for p in peers:
        pl.semaphore_signal(barrier, inc=1, device_id=p, device_id_type=MESH)
    slot_iota = lax.broadcasted_iota(jnp.int32, (1, TOK), 1)
    lab[c, 0, 0] = jnp.where(slot_iota < counts[0], labels[...], -1)
    loads[0].wait()
    loads[1].wait()
    pl.semaphore_wait(barrier, len(peers))

    for s in FAR:
        d = ZORD[s]
        t = ZPOS[(NZ - d) % NZ]
        send(rg.at[0, 0], rg.at[0, t], rzs.at[s], rzr.at[t], dev(dz=d))
    send(actv.at[mine], actv.at[mine], exs.at[0], exr.at[0], dev(core=oc))
    for s in FAR:
        d = ZORD[s]
        t = ZPOS[(NZ - d) % NZ]
        send(lab.at[c, 0, 0], lab.at[c, 0, t], bzs.at[s], bzr.at[t], dev(dz=d))
    for s in FAR:
        d = ZORD[s]
        t = ZPOS[(NZ - d) % NZ]
        for k, core in enumerate((c, oc)):
            cols = pl.ds(pl.multiple_of(core * H, H), H)
            send(left.at[:, cols], lg.at[c, 0, t], lzs.at[k, s], lzr.at[k, t], dev(dz=d, core=core))
    send(left.at[:, pl.ds(pl.multiple_of(oc * H, H), H)], lg.at[c, 0, 0], lzs.at[1, 0], lzr.at[1, 0], dev(core=oc))
    lg[c, 0, 0] = left[:, pl.ds(pl.multiple_of(c * H, H), H)]

    cen[mine, :] = (actv[mine, :].astype(F32) - mean[...]).astype(BF16)

    for g, (first, number) in enumerate(GROUPS):
        for s in range(first, first + number):
            if s:
                got(rg.at[0, s], rzr.at[s])
        for s in (3, 2, 1):
            d = XORD[s]
            t = XPOS[(NX - d) % NX]
            zs = pl.ds(first, number)
            send(rg.at[0, zs], rg.at[t, zs], rxs.at[s, g], rxr.at[t, g], dev(dx=d))
    got(actv.at[theirs], exr.at[0])
    cen[theirs, :] = (actv[theirs, :].astype(F32) - mean[...]).astype(BF16)

    for s in range(1, NZ):
        got(lab.at[c, 0, s], bzr.at[s])
    for s in (3, 2, 1):
        d = XORD[s]
        t = XPOS[(NX - d) % NX]
        send(lab.at[c, 0], lab.at[c, t], bxs.at[s], bxr.at[t], dev(dx=d))

    def chunk(k):
        for xs in (2 * k, 2 * k + 1):
            for g, (first, number) in enumerate(GROUPS):
                if xs:
                    zs = pl.ds(first, number)
                    got(rg.at[xs, zs], rxr.at[xs, g])
        rmat = rg[2 * k : 2 * k + 2].astype(F32).reshape(K2, D).astype(BF16)
        part = lax.dot_general(cen[...], rmat, (((1,), (1,)), ((), ())), preferred_element_type=F32)
        pbuf[k] = part.astype(BF16)
        for s in FAR:
            d = ZORD[s]
            t = ZPOS[(NY - d) % NY]
            rows = pl.ds(pl.multiple_of(lax.rem(y + d, NY) * YB, YB), YB)
            send(pbuf.at[k, rows], prx.at[k, t], pss.at[k, s], psr.at[k, t], dev(dy=d))

    own_rows = pl.ds(pl.multiple_of(y * YB, YB), YB)

    def reduce(k):
        total = pbuf[k, own_rows, :].astype(F32)
        for s in range(1, NY):
            got(prx.at[k, s], psr.at[k, s])
            total = total + prx[k, s].astype(F32)
        cbuf[c, k, own_rows, :] = total.astype(BF16)
        for s in FAR:
            d = ZORD[s]
            t = ZPOS[(NY - d) % NY]
            send(cbuf.at[c, k, own_rows], cbuf.at[c, k, own_rows], css.at[k, s], csr.at[k, t], dev(dy=d))

    def gathered(k):
        for s in range(1, NY):
            rows = pl.ds(pl.multiple_of(lax.rem(y + ZORD[s], NY) * YB, YB), YB)
            got(cbuf.at[c, k, rows], csr.at[k, s])
        send(cbuf.at[c, k], cbuf.at[c, k], exs.at[2 + k], exr.at[2 + k], dev(core=oc))

    chunk(0)
    got(lg.at[oc, 0, 0], lzr.at[1, 0])
    for s in range(1, NZ):
        got(lg.at[c, 0, s], lzr.at[0, s])
        got(lg.at[oc, 0, s], lzr.at[1, s])
    for s in (3, 2, 1):
        d = XORD[s]
        t = XPOS[(NX - d) % NX]
        send(lg.at[:, 0], lg.at[:, t], lxs.at[s], lxr.at[t], dev(dx=d))
    chunk(1)

    for s in range(1, NX):
        got(lab.at[c, s], bxr.at[s])
    send(lab.at[c], lab.at[c], exs.at[1], exr.at[1], dev(core=oc))
    got(lab.at[oc], exr.at[1])
    own_class = dp * RD + lax.broadcasted_iota(jnp.int32, (RD, TOK), 0)
    hits, valid = jnp.zeros((RD, TOK), F32), jnp.zeros((1, TOK), F32)
    for k in range(2):
        for xs in range(NX):
            for zs in range(NZ):
                row = lab[k, xs, zs]
                hits = hits + (row == own_class).astype(F32)
                valid = valid + (row >= 0).astype(F32)
    own_counts = jnp.sum(hits, axis=1, keepdims=True)
    grand = jnp.sum(valid, axis=1, keepdims=True)
    tokens = jnp.concatenate([lab[0, 0, 0], lab[1, 0, 0]], axis=1)
    for xs in range(NX):
        for zs in range(NZ):
            r = lax.broadcasted_iota(jnp.int32, (2 * RD, T2), 0)
            owner = lax.rem(z + ZORD[zs], NZ) * NX + lax.rem(x + XORD[xs], NX)
            at = (xs * NZ + zs) * 2 * RD
            oh[at : at + 2 * RD, :] = (owner * (2 * RD) + r == tokens).astype(F32).astype(BF16)

    reduce(0)
    for s in range(1, NX):
        got(lg.at[:, s], lxr.at[s])
    for k in range(2):
        lm[k * 256 : (k + 1) * 256, :] = lg[k].astype(F32).reshape(256, H).astype(BF16)
    reduce(1)
    gathered(0)
    gathered(1)
    for k in range(2):
        got(cbuf.at[oc, k], exr.at[2 + k])

    coords = jnp.concatenate([cbuf[0, 0], cbuf[0, 1], cbuf[1, 0], cbuf[1, 1]], axis=1)
    for q in range(QN):
        cols = slice(q * QW, (q + 1) * QW)
        corr = jnp.dot(coords, lm[:, cols], preferred_element_type=F32)
        acols = pl.ds(pl.multiple_of(c * H + q * QW, QW), QW)
        er[:, cols] = (actv[:, acols].astype(F32) - corr).astype(BF16)
        sums = jnp.dot(oh[...], er[:, cols], preferred_element_type=F32)
        s0[:, cols] = sums[:128]
        txs[:, cols] = jnp.sum(sums, axis=0, keepdims=True)
        for s in (3, 2, 1):
            d = XORD[s]
            t = XPOS[(NX - d) % NX]
            sxs[q, s] = sums[s * 128 : (s + 1) * 128].astype(BF16)
            send(sxs.at[q, s], sxr.at[q, t], xxs.at[q, s], xxr.at[q, t], dev(dx=d))
    for s in (3, 2, 1):
        d = XORD[s]
        t = XPOS[(NX - d) % NX]
        send(txs, txr.at[t], xxs.at[QN, s], xxr.at[QN, t], dev(dx=d))
    half = pl.ds(pl.multiple_of(c * H, H), H)
    keep = pltpu.make_async_copy(er.at[mine], out.at[:, half], loc.at[2])
    keep.start()
    send(er.at[theirs], out.at[:, half], exs.at[4], exr.at[4], dev(core=oc))

    for q in range(QN):
        cols = slice(q * QW, (q + 1) * QW)
        total = s0[:, cols]
        for s in range(1, NX):
            got(sxr.at[q, s], xxr.at[q, s])
            total = total + sxr[q, s].astype(F32)
        s0[:, cols] = total
    tot = txs[...]
    for s in range(1, NX):
        got(txr.at[s], xxr.at[QN, s])
        tot = tot + txr[s]
    tzs[...] = tot

    for s in FAR + (0,):
        d = ZORD[s]
        t = ZPOS[(NZ - d) % NZ]
        for core in range(2):
            at = (s * 2 + core) * RD
            szs[s, core] = s0[at : at + RD, :].astype(BF16)
        for k, core in enumerate((c, oc)):
            if s == 0 and k == 0:
                continue
            send(szs.at[s, core], szr.at[c, t], zzs.at[0, k, s], zzr.at[0, k, t], dev(dz=d, core=core))
            send(tzs, tzr.at[c, t], zzs.at[1, k, s], zzr.at[1, k, t], dev(dz=d, core=core))
    szr[c, 0] = szs[0, c]
    tzr[c, 0] = tot
    for s in range(NZ):
        for k, core in enumerate((c, oc)):
            if s == 0 and k == 0:
                continue
            got(szr.at[core, s], zzr.at[0, k, s])
            got(tzr.at[core, s], zzr.at[1, k, s])
    scale = 1.0 / jnp.sqrt(jnp.maximum(own_counts, 1.0))
    for h in range(2):
        class_sums, totals = szr[h, 0].astype(F32), tzr[h, 0]
        for s in range(1, NZ):
            class_sums = class_sums + szr[h, s].astype(F32)
            totals = totals + tzr[h, s]
        feature_mean = totals / grand
        scores[:, h * H : (h + 1) * H] = (class_sums - own_counts * feature_mean) * scale
    lane = lax.broadcasted_iota(jnp.int32, (RD, RD), 1)
    row = lax.broadcasted_iota(jnp.int32, (RD, RD), 0)
    cnt[...] = jnp.sum(jnp.where(lane == row, own_counts, 0.0), axis=0, keepdims=True).astype(jnp.int32)

    keep.wait()
    got(out.at[:, pl.ds(pl.multiple_of(oc * H, H), H)], exr.at[4])
    for cp in sent:
        cp.wait_send()


def per_device(acts, mean_vec, left_factor, right_factor, labels, counts):
    dma = pltpu.SemaphoreType.DMA
    ng = len(GROUPS)
    vm, hbm = pl.BlockSpec(memory_space=pltpu.VMEM), pl.BlockSpec(memory_space=pl.ANY)
    erased, scores, cnt = pl.pallas_call(
        kernel,
        out_shape=(
            jax.ShapeDtypeStruct((TOK, D), BF16),
            jax.ShapeDtypeStruct((RD, D), F32),
            jax.ShapeDtypeStruct((1, RD), jnp.int32),
        ),
        in_specs=[hbm, vm, vm, hbm, vm, pl.BlockSpec(memory_space=pltpu.SMEM)],
        out_specs=(hbm, vm, vm),
        scratch_shapes=[
            pltpu.VMEM((T2, D), BF16),
            pltpu.VMEM((T2, D), BF16),
            pltpu.VMEM((NX, NZ, RD, D), BF16),
            pltpu.VMEM((2, NX, NZ, RD, H), BF16),
            pltpu.VMEM((C, H), BF16),
            pltpu.VMEM((2, NX, NZ, 1, TOK), jnp.int32),
            pltpu.VMEM((2, T2, K2), BF16),
            pltpu.VMEM((2, NY, YB, K2), BF16),
            pltpu.VMEM((2, 2, T2, K2), BF16),
            pltpu.VMEM((C, T2), BF16),
            pltpu.VMEM((T2, H), BF16),
            pltpu.VMEM((QN, NX, 128, QW), BF16),
            pltpu.VMEM((QN, NX, 128, QW), BF16),
            pltpu.VMEM((128, H), F32),
            pltpu.VMEM((1, H), F32),
            pltpu.VMEM((NX, 1, H), F32),
            pltpu.VMEM((NZ, 2, RD, H), BF16),
            pltpu.VMEM((2, NZ, RD, H), BF16),
            pltpu.VMEM((1, H), F32),
            pltpu.VMEM((2, NZ, 1, H), F32),
            dma((3,)),
            dma((NZ,)), dma((NZ,)),
            dma((NX, ng)), dma((NX, ng)),
            dma((2, NZ)), dma((2, NZ)),
            dma((NX,)), dma((NX,)),
            dma((NZ,)), dma((NZ,)),
            dma((NX,)), dma((NX,)),
            dma((5,)), dma((5,)),
            dma((2, NY)), dma((2, NY)),
            dma((2, NY)), dma((2, NY)),
            dma((QN + 1, NX)), dma((QN + 1, NX)),
            dma((2, 2, NZ)), dma((2, 2, NZ)),
        ],
        compiler_params=pltpu.CompilerParams(
            collective_id=0, has_side_effects=True, vmem_limit_bytes=40 << 20
        ),
        cost_estimate=pl.CostEstimate(flops=6 * 256 * 1024 * 512, bytes_accessed=4 << 20, transcendentals=0),
    )(
        acts,
        mean_vec.reshape(1, D),
        left_factor,
        right_factor,
        labels.reshape(1, TOK),
        counts,
    )
    return erased, scores, cnt.reshape(RD)


def solution(mesh):
    return jax.shard_map(
        per_device,
        mesh=mesh,
        in_specs=(
            P("dp", "tensor"),
            P("tensor"),
            P("dp", "tensor"),
            P("dp", "tensor"),
            P("dp"),
            P("dp"),
        ),
        out_specs=(P("dp", "tensor"), P("dp", "tensor"), P("dp")),
        check_vma=False,
    )
```

time: 392 us -> 67.2 us (0.17)
  waiting for transfers between devices: 210 us -> 0 us
  blocking collectives: 156 us -> 0 us
  Pallas kernels: 0 us -> 60.5 us
  between operations: 15.2 us -> 1.32 us
  matrix products: 5.59 us -> 0 us
    psum x2 -> x0, blocking collectives: 156 us -> none  [the longest x1 126 us: per_device(): counts_all, totals_all = lax.psum((count_part, feature_part), 'dp')]
    all_gather x2 -> x0, waiting for transfers between devices: 141 us -> none  [the longest x1 90.4 us: per_device(): lax.all_gather(right_factor, 'dp', axis=0, tiled=True)]
    unnamed x4 -> x0, waiting for transfers between devices: 68.1 us -> none
    pallas_call x0 -> x1, Pallas kernels: none -> 60.5 us  [per_device(): pl.pallas_call(kernel, out_shape=(jax.ShapeDtypeStruct((TOK, D), BF16), j...]
    dot_general x4 -> x0, matrix products: 5.59 us -> none  [the longest x1 1.87 us: per_device(): lax.dot_general(onehot, erased, (((0,), (0,)), ((), ())), preferred_eleme...]
  transfers between devices with their start and end apart: 3 -> 0, of which waited for: 3 -> 0; matrix products, arithmetic and copies ran while one was open for 1% -> 0% of each run, Pallas kernels for 0% -> 0%
where the time goes in v1:
time: 67.2 us; the launch traced here: 66.9 us
  Pallas kernels  60.5 us (90%)
  local copies, waits for them, and re-layouts  5.07 us (8%)
  between operations  1.32 us (2%)
    pallas_call x1, Pallas kernels, per_device(): pl.pallas_call(kernel, out_shape=(jax.ShapeDtypeStruct((TOK, D), BF16), j...  60.5 us
    unnamed x13, local copies, waits for them, and re-layouts  5.07 us

profile of v1, /device:TPU:1, one launch (start us, length us, event | category | flops | bytes accessed | tf_op | source)
XLA Modules:
  0.0 66.9 jit_solution(4138131011906710750)
XLA Ops:
  0.6 0.0 copy-start.3
  1.3 0.0 copy-start.4
  1.3 0.0 copy-done.3
  1.3 0.7 copy-done.4
  2.0 0.0 copy-start
  2.0 1.0 %copy-done = bf16[256,1024]{1,0:T(8,128)(2,1)S(1)} copy-done((bf16[256,1024]{1,0:T(8,128)(2,1)S(1)}, bf16[256,1024]{1,0:T(8,128)(2,1)}, u32[]{:S(2)}) %copy-start) | copy-done | bytes 524312
  3.0 0.0 copy-start.1
  3.0 0.7 %copy-done.1 = bf16[8,1024]{1,0:T(8,128)(2,1)S(1)} copy-done((bf16[8,1024]{1,0:T(8,128)(2,1)S(1)}, bf16[8,1024]{1,0:T(8,128)(2,1)}, u32[]{:S(2)}) %copy-start.1) | copy-done | bytes 16408
  3.7 0.0 copy-start.2
  3.7 0.7 %copy-done.2 = bf16[8,1024]{1,0:T(8,128)(2,1)S(1)} copy-done((bf16[8,1024]{1,0:T(8,128)(2,1)S(1)}, bf16[8,1024]{1,0:T(8,128)(2,1)}, u32[]{:S(2)}) %copy-start.2) | copy-done | bytes 16408
  4.5 60.5 %shard_map.85 = (bf16[256,1024]{1,0:T(8,128)(2,1)S(1)}, f32[8,1024]{1,0:T(8,128)S(1)}, s32[1,8]{1,0:T(1,128)S(1)}) custom-call(bf16[256,1024]{1,0:T(8,128)(2,1)S(1)} %copy-done, f32[1,1024]{1,0:T(1,128)S(1)} %bitcast.3, bf16[8,1024]{1,0:T(8,128)(2,1)S(1)} %copy-done.1, bf16[8,1024]{1,0:T(8,128)(2,1)S(1)} %copy-done.2, s32[1,256]{1,0:T(1,128)S(1)} %bitcast.4, ...), custom_call_target="tpu_custom_call" | custom-call | flops 805306368 | bytes 4194304 | tf_op jit(solution)/shard_map/pallas_call | solution.py:272
  65.0 0.8 %copy.13 = bf16[256,1024]{1,0:T(8,128)(2,1)} copy(bf16[256,1024]{1,0:T(8,128)(2,1)S(1)} %get-tuple-element.12) | data formatting | bytes 1048576
  65.8 0.6 copy.14
  66.4 0.5 copy.15
Async XLA Ops:
  0.6 0.7 %copy-start.3 = (f32[1024]{0:T(1024)S(1)}, f32[1024]{0:T(1024)}, u32[]{:S(2)}) copy-start(f32[1024]{0:T(1024)} %param.7) | copy-start | bytes 12292
  1.3 0.7 %copy-start.4 = (s32[256]{0:T(256)S(1)}, s32[256]{0:T(256)}, u32[]{:S(2)}) copy-start(s32[256]{0:T(256)} %param.10) | copy-start | bytes 3076
  2.0 1.0 %copy-start = (bf16[256,1024]{1,0:T(8,128)(2,1)S(1)}, bf16[256,1024]{1,0:T(8,128)(2,1)}, u32[]{:S(2)}) copy-start(bf16[256,1024]{1,0:T(8,128)(2,1)} %acts.1) | copy-start | bytes 1572868
  3.0 0.7 %copy-start.1 = (bf16[8,1024]{1,0:T(8,128)(2,1)S(1)}, bf16[8,1024]{1,0:T(8,128)(2,1)}, u32[]{:S(2)}) copy-start(bf16[8,1024]{1,0:T(8,128)(2,1)} %left.1) | copy-start | bytes 49156
  3.7 0.7 %copy-start.2 = (bf16[8,1024]{1,0:T(8,128)(2,1)S(1)}, bf16[8,1024]{1,0:T(8,128)(2,1)}, u32[]{:S(2)}) copy-start(bf16[8,1024]{1,0:T(8,128)(2,1)} %right.1) | copy-start | bytes 49156

commit v2 on v0

v2 whole, which is shorter than its diff:
```python
import functools

import jax
import jax.numpy as jnp
from jax import lax
from jax.experimental import pallas as pl
from jax.experimental.pallas import tpu as pltpu
from jax.sharding import PartitionSpec as P

MESH = pl.DeviceIdType.MESH
F32, BF16, I32 = jnp.float32, jnp.bfloat16, jnp.int32
C = 512
NZ, NX, NY = 8, 4, 8
ZORD = (0, 1, 7, 2, 6, 3, 5, 4)
XORD = (0, 1, 3, 2)
ZBACK = tuple(ZORD.index((NZ - d) % NZ) for d in ZORD)
XBACK = tuple(XORD.index((NX - d) % NX) for d in XORD)
NEAR, FAR = (1, 2, 3, 4, 5, 6, 7), (7, 6, 5, 4, 3, 2, 1)
XFIRST = (2, 3, 1)
GROUPS = ((0, 2), (2, 2), (4, 2), (6, 2))
TOK, D, RD = 256, 1024, 8
T2, H, K2 = 512, 512, 128
QN = 2
QW = H // QN
YB = T2 // NY
VLIM = 63 << 20


def kernel(
    acts, mean, left, right, labels, counts,
    out, scores, cnt,
    meanv, labv, cntv, actv, cen, rg, lg, lo, lm, lab, pbuf, prx, cbuf, oh, er,
    sxs, sxr, s0, txs, txr, szs, szr, tzs, tzr, fin,
    loc, rzs, rzr, rxs, rxr, lzs, lzr, lxs, lxr, bzs, bzr, bxs, bxr, exs, exr,
    pss, psr, css, csr, fcs, fcr, xxs, xxr, zzs, zzr,
):
    dp, y = lax.axis_index("dp"), lax.axis_index("tensor")
    c, x, z = lax.rem(dp, 2), lax.rem(dp // 2, NX), dp // (2 * NX)
    oc = 1 - c

    def dev(dz=0, dx=0, dy=0, core=None):
        core = c if core is None else core
        zz, xx, yy = lax.rem(z + dz, NZ), lax.rem(x + dx, NX), lax.rem(y + dy, NY)
        return ((zz * NX + xx) * 2 + core, yy)

    other = dev(core=oc)

    def send(src, dst, ss, rs, to):
        pltpu.make_async_remote_copy(
            src_ref=src,
            dst_ref=dst,
            send_sem=ss[0].at[ss[1]],
            recv_sem=rs[0].at[rs[1]],
            device_id=to,
            device_id_type=MESH,
        ).start()

    def got(ref, rs):
        sem = rs[0].at[rs[1]]
        pltpu.make_async_remote_copy(
            src_ref=ref, dst_ref=ref, send_sem=sem, recv_sem=sem, device_id=other, device_id_type=MESH
        ).wait_recv()

    def gone(ref, ss):
        sem = ss[0].at[ss[1]]
        pltpu.make_async_remote_copy(
            src_ref=ref, dst_ref=ref, send_sem=sem, recv_sem=sem, device_id=other, device_id_type=MESH
        ).wait_send()

    def along_z(order, src, dst, ss, rs):
        for s in order:
            send(src(s), dst(ZBACK[s]), ss, rs(ZBACK[s]), dev(dz=ZORD[s]))

    def along_y(order, src, dst, ss, rs):
        for s in order:
            send(src(s), dst(ZBACK[s]), ss, rs(ZBACK[s]), dev(dy=ZORD[s]))

    def along_x(src, dst, ss, rs):
        for s in XFIRST:
            send(src(s), dst(XBACK[s]), ss, rs(XBACK[s]), dev(dx=XORD[s]))

    mine, theirs = pl.ds(0, TOK), pl.ds(TOK, TOK)
    loads = [
        pltpu.make_async_copy(src, dst, loc.at[i])
        for i, (src, dst) in enumerate(
            (
                (right, rg.at[0, 0]),
                (acts, actv.at[mine]),
                (mean, meanv),
                (labels, labv),
                (counts, cntv),
                (left, lg.at[0, 0]),
            )
        )
    ]
    for cp in loads:
        cp.start()

    barrier = pltpu.get_barrier_semaphore()
    peers = [dev(dz=ZORD[s]) for s in FAR] + [dev(dy=ZORD[s]) for s in FAR]
    peers += [dev(dx=d) for d in (2, 1, 3)] + [other]
    for p in peers:
        pl.semaphore_signal(barrier, inc=1, device_id=p, device_id_type=MESH)
    loads[0].wait()
    pl.semaphore_wait(barrier, len(peers))

    group_of = {s: g for g, (first, number) in enumerate(GROUPS) for s in range(first, first + number)}
    along_z(NEAR, lambda s: rg.at[0, 0], lambda t: rg.at[0, t], (rzs, 0), lambda t: (rzr, group_of[t]))
    loads[1].wait()
    send(actv.at[mine], actv.at[theirs], (exs, 0), (exr, 0), other)
    for cp in loads[2:]:
        cp.wait()
    cen[mine, :] = (actv[mine, :].astype(F32) - meanv[...]).astype(BF16)
    slot_iota = lax.broadcasted_iota(I32, (1, TOK), 1)
    lab[0, 0, 0] = jnp.where(slot_iota < cntv[...], labv[...], -1)

    for g, (first, number) in enumerate(GROUPS):
        fresh = max(first, 1)
        got(rg.at[0, fresh : first + number], (rzr, g))
        zs = pl.ds(first, number)
        along_x(lambda s: rg.at[0, zs], lambda t: rg.at[t, zs], (rxs, 0), lambda t: (rxr, t))

    along_z(NEAR, lambda s: lab.at[0, 0, 0], lambda t: lab.at[0, 0, t], (bzs, 0), lambda t: (bzr, 0))
    along_z(NEAR, lambda s: lg.at[0, 0], lambda t: lg.at[0, t], (lzs, 0), lambda t: (lzr, 0))
    got(actv.at[theirs], (exr, 0))
    cen[theirs, :] = (actv[theirs, :].astype(F32) - meanv[...]).astype(BF16)

    def block(s, turn=0):
        return pl.ds(pl.multiple_of(lax.rem(y + ZORD[s] + turn, NY) * YB, YB), YB)

    def chunk(k):
        for xs in (2 * k, 2 * k + 1):
            if xs:
                got(rg.at[xs], (rxr, xs))
        rmat = rg[2 * k : 2 * k + 2].astype(F32).reshape(K2, D).astype(BF16)
        part = lax.dot_general(cen[...], rmat, (((1,), (1,)), ((), ())), preferred_element_type=F32)
        pbuf[k] = part.astype(BF16)
        along_y(FAR, lambda s: pbuf.at[k, block(s)], lambda t: prx.at[k, t], (pss, k), lambda t: (psr, k))

    def across(k, s):
        ref, there = cbuf.at[0, k, block(s)], cbuf.at[1, k, block(s, NY // 2)]
        send(ref, there, (fcs, k), (fcr, k), other)

    def reduce(k):
        total = pbuf[k, block(0), :].astype(F32)
        got(prx.at[k, 1:NY], (psr, k))
        for s in range(1, NY):
            total = total + prx[k, s].astype(F32)
        own = cbuf.at[0, k, block(0)]
        own[...] = total.astype(BF16)
        along_y(FAR, lambda s: own, lambda t: own, (css, k), lambda t: (csr, k * NY + t))
        across(k, 0)

    def gathered(k):
        for s in range(1, NY):
            got(cbuf.at[0, k, block(s)], (csr, k * NY + s))
            across(k, s)

    chunk(0)
    chunk(1)
    got(lab.at[0, 0, 1:NZ], (bzr, 0))
    along_x(lambda s: lab.at[0, 0], lambda t: lab.at[0, t], (bxs, 0), lambda t: (bxr, 0))
    got(lg.at[0, 1:NZ], (lzr, 0))
    along_x(lambda s: lg.at[0], lambda t: lg.at[t], (lxs, 0), lambda t: (lxr, 0))

    reduce(0)
    reduce(1)

    got(lab.at[0, 1:NX], (bxr, 0))
    send(lab.at[0], lab.at[1], (exs, 1), (exr, 1), other)
    got(lg.at[1:NX], (lxr, 0))
    half, their_half = pl.ds(pl.multiple_of(c * H, H), H), pl.ds(pl.multiple_of(oc * H, H), H)
    send(lg.at[:, :, :, their_half], lo, (exs, 2), (exr, 2), other)
    lm[0:256, :] = lg[:, :, :, half].astype(F32).reshape(256, H).astype(BF16)
    got(lab.at[1], (exr, 1))
    chip = z * NX + x
    own_class = chip * (2 * RD) + lax.broadcasted_iota(I32, (2 * RD, TOK), 0)
    hits, valid = jnp.zeros((2 * RD, TOK), F32), jnp.zeros((1, TOK), F32)
    for k in range(2):
        for xs in range(NX):
            for zs in range(NZ):
                row = lab[k, xs, zs]
                hits = hits + (row == own_class).astype(F32)
                valid = valid + (row >= 0).astype(F32)
    own_counts = jnp.sum(hits, axis=1, keepdims=True)
    grand = jnp.sum(valid, axis=1, keepdims=True)
    tokens = jnp.concatenate([lab[0, 0, 0], lab[1, 0, 0]], axis=1)
    for xs in range(NX):
        for zs in range(NZ):
            r = lax.broadcasted_iota(I32, (2 * RD, T2), 0)
            owner = lax.rem(z + ZORD[zs], NZ) * NX + lax.rem(x + XORD[xs], NX)
            at = (xs * NZ + zs) * 2 * RD
            oh[at : at + 2 * RD, :] = (owner * (2 * RD) + r == tokens).astype(F32).astype(BF16)

    gathered(0)
    got(lo, (exr, 2))
    lm[256:512, :] = lo[...].astype(F32).reshape(256, H).astype(BF16)
    gathered(1)
    for k in range(2):
        got(cbuf.at[1, k], (fcr, k))

    coords = jnp.concatenate([cbuf[0, 0], cbuf[0, 1], cbuf[1, 0], cbuf[1, 1]], axis=1)
    for q in range(QN):
        cols = slice(q * QW, (q + 1) * QW)
        corr = jnp.dot(coords, lm[:, cols], preferred_element_type=F32)
        acols = pl.ds(pl.multiple_of(c * H + q * QW, QW), QW)
        er[:, cols] = (actv[:, acols].astype(F32) - corr).astype(BF16)
        sums = jnp.dot(oh[...], er[:, cols], preferred_element_type=F32)
        s0[:, cols] = sums[:128]
        txs[:, cols] = jnp.sum(sums, axis=0, keepdims=True)
        for s in range(1, NX):
            sxs[q, s] = sums[s * 128 : (s + 1) * 128].astype(BF16)
        along_x(lambda s: sxs.at[q, s], lambda t: sxr.at[q, t], (xxs, q), lambda t: (xxr, q))
    along_x(lambda s: txs, lambda t: txr.at[t], (xxs, QN), lambda t: (xxr, QN))
    keep = pltpu.make_async_copy(er.at[mine], out.at[:, half], loc.at[6])
    keep.start()
    send(er.at[theirs], out.at[:, half], (exs, 3), (exr, 3), other)

    for q in range(QN):
        cols = slice(q * QW, (q + 1) * QW)
        total = s0[:, cols]
        got(sxr.at[q, 1:NX], (xxr, q))
        for s in range(1, NX):
            total = total + sxr[q, s].astype(F32)
        for s in NEAR:
            szs[q, s] = total[s * 2 * RD : (s + 1) * 2 * RD, :].astype(BF16)
        s0[0 : 2 * RD, cols] = total[0 : 2 * RD]
        along_z(FAR, lambda s: szs.at[q, s], lambda t: szr.at[q, t], (zzs, q), lambda t: (zzr, q))
    total = txs[...]
    got(txr.at[1:NX], (xxr, QN))
    for s in range(1, NX):
        total = total + txr[s]
    tzs[...] = total
    along_z(FAR, lambda s: tzs, lambda t: tzr.at[t], (zzs, QN), lambda t: (zzr, QN))

    scale = 1.0 / jnp.sqrt(jnp.maximum(own_counts, 1.0))
    got(szr.at[0, 1:NZ], (zzr, 0))
    got(szr.at[1, 1:NZ], (zzr, 1))
    got(tzr.at[1:NZ], (zzr, QN))
    for s in range(1, NZ):
        total = total + tzr[s]
    feature_mean = total / grand
    for q in range(QN):
        cols = slice(q * QW, (q + 1) * QW)
        class_sums = s0[0 : 2 * RD, cols]
        for s in range(1, NZ):
            class_sums = class_sums + szr[q, s].astype(F32)
        fin[:, cols] = (class_sums - own_counts * feature_mean[:, cols]) * scale
    own_fin = fin.at[pl.ds(pl.multiple_of(c * RD, RD), RD)]
    send(fin.at[pl.ds(pl.multiple_of(oc * RD, RD), RD)], scores.at[:, half], (exs, 4), (exr, 4), other)
    put = pltpu.make_async_copy(own_fin, scores.at[:, half], loc.at[7])
    put.start()
    lane = lax.broadcasted_iota(I32, (2 * RD, RD), 1)
    row = lax.broadcasted_iota(I32, (2 * RD, RD), 0)
    cnt[...] = jnp.sum(jnp.where(lane + c * RD == row, own_counts, 0.0), axis=0, keepdims=True).astype(I32)

    keep.wait()
    gone(rg.at[0, 1:NZ], (rzs, 0))
    gone(rg.at[1:NX], (rxs, 0))
    gone(lab.at[0, 0, 1:NZ], (bzs, 0))
    gone(lg.at[0, 1:NZ], (lzs, 0))
    gone(lab.at[0, 1:NX], (bxs, 0))
    gone(lg.at[1:NX], (lxs, 0))
    gone(actv.at[mine], (exs, 0))
    gone(lab.at[0], (exs, 1))
    gone(lo, (exs, 2))
    gone(er.at[theirs], (exs, 3))
    for k in range(2):
        gone(prx.at[k, 1:NY], (pss, k))
        gone(prx.at[k, 1:NY], (css, k))
        gone(cbuf.at[0, k], (fcs, k))
    for q in range(QN):
        gone(sxr.at[q, 1:NX], (xxs, q))
        gone(szr.at[q, 1:NZ], (zzs, q))
    gone(txr.at[1:NX], (xxs, QN))
    gone(tzr.at[1:NZ], (zzs, QN))
    gone(own_fin, (exs, 4))
    got(er.at[theirs], (exr, 3))
    put.wait()
    got(own_fin, (exr, 4))


def hand_out(erased, scores, cnt, erased_out, scores_out, cnt_out, sems):
    pairs = ((erased, erased_out), (scores, scores_out), (cnt, cnt_out))
    copies = [pltpu.make_async_copy(a, b, sems.at[i]) for i, (a, b) in enumerate(pairs)]
    for cp in copies:
        cp.start()
    for cp in copies:
        cp.wait()


def per_device(acts, mean_vec, left_factor, right_factor, labels, counts):
    dma = pltpu.SemaphoreType.DMA
    ng = len(GROUPS)
    vm, anywhere = pl.BlockSpec(memory_space=pltpu.VMEM), pl.BlockSpec(memory_space=pl.ANY)
    hbm = pl.BlockSpec(memory_space=pltpu.HBM)
    shapes = (
        jax.ShapeDtypeStruct((TOK, D), BF16),
        jax.ShapeDtypeStruct((RD, D), F32),
        jax.ShapeDtypeStruct((1, RD), I32),
    )
    results = pl.pallas_call(
        kernel,
        out_shape=shapes,
        in_specs=[hbm] * 6,
        out_specs=(anywhere, anywhere, vm),
        scratch_shapes=[
            pltpu.VMEM((1, D), F32),
            pltpu.VMEM((1, TOK), I32),
            pltpu.VMEM((1, 1), I32),
            pltpu.VMEM((T2, D), BF16),
            pltpu.VMEM((T2, D), BF16),
            pltpu.VMEM((NX, NZ, RD, D), BF16),
            pltpu.VMEM((NX, NZ, RD, D), BF16),
            pltpu.VMEM((NX, NZ, RD, H), BF16),
            pltpu.VMEM((C, H), BF16),
            pltpu.VMEM((2, NX, NZ, 1, TOK), I32),
            pltpu.VMEM((2, T2, K2), BF16),
            pltpu.VMEM((2, NY, YB, K2), BF16),
            pltpu.VMEM((2, 2, T2, K2), BF16),
            pltpu.VMEM((C, T2), BF16),
            pltpu.VMEM((T2, H), BF16),
            pltpu.VMEM((QN, NX, 128, QW), BF16),
            pltpu.VMEM((QN, NX, 128, QW), BF16),
            pltpu.VMEM((128, H), F32),
            pltpu.VMEM((1, H), F32),
            pltpu.VMEM((NX, 1, H), F32),
            pltpu.VMEM((QN, NZ, 2 * RD, QW), BF16),
            pltpu.VMEM((QN, NZ, 2 * RD, QW), BF16),
            pltpu.VMEM((1, H), F32),
            pltpu.VMEM((NZ, 1, H), F32),
            pltpu.VMEM((2 * RD, H), F32),
            dma((8,)),
            dma((1,)), dma((ng,)),
            dma((1,)), dma((NX,)),
            dma((1,)), dma((1,)),
            dma((1,)), dma((1,)),
            dma((1,)), dma((1,)),
            dma((1,)), dma((1,)),
            dma((5,)), dma((5,)),
            dma((2,)), dma((2,)),
            dma((2,)), dma((2 * NY,)),
            dma((2,)), dma((2,)),
            dma((QN + 1,)), dma((QN + 1,)),
            dma((QN + 1,)), dma((QN + 1,)),
        ],
        compiler_params=pltpu.CompilerParams(
            collective_id=0, has_side_effects=True, vmem_limit_bytes=VLIM
        ),
        cost_estimate=pl.CostEstimate(flops=6 * 256 * 1024 * 512, bytes_accessed=4 << 20, transcendentals=0),
    )(
        acts,
        mean_vec.reshape(1, D),
        left_factor,
        right_factor,
        labels.reshape(1, TOK),
        counts.reshape(1, 1),
    )
    erased, scores, cnt = pl.pallas_call(
        hand_out,
        out_shape=shapes,
        in_specs=[vm] * 3,
        out_specs=(hbm,) * 3,
        scratch_shapes=[dma((3,))],
    )(*results)
    return erased, scores, cnt.reshape(RD)


def solution(mesh):
    return jax.shard_map(
        per_device,
        mesh=mesh,
        in_specs=(
            P("dp", "tensor"),
            P("tensor"),
            P("dp", "tensor"),
            P("dp", "tensor"),
            P("dp"),
            P("dp"),
        ),
        out_specs=(P("dp", "tensor"), P("dp", "tensor"), P("dp")),
        check_vma=False,
    )
```

time: 392 us -> 59 us (0.15)
  waiting for transfers between devices: 210 us -> 0 us
  blocking collectives: 156 us -> 0 us
  Pallas kernels: 0 us -> 57.5 us
  between operations: 15.2 us -> 1.29 us
  matrix products: 5.59 us -> 0 us
    psum x2 -> x0, blocking collectives: 156 us -> none  [the longest x1 126 us: per_device(): counts_all, totals_all = lax.psum((count_part, feature_part), 'dp')]
    all_gather x2 -> x0, waiting for transfers between devices: 141 us -> none  [the longest x1 90.4 us: per_device(): lax.all_gather(right_factor, 'dp', axis=0, tiled=True)]
    unnamed x4 -> x0, waiting for transfers between devices: 68.1 us -> none
    pallas_call x0 -> x2, Pallas kernels: none -> 57.5 us  [the longest x1 55.6 us: per_device(): pl.pallas_call(kernel, out_shape=shapes, in_specs=[hbm] * 6, out_specs=(a...]
    dot_general x4 -> x0, matrix products: 5.59 us -> none  [the longest x1 1.87 us: per_device(): lax.dot_general(onehot, erased, (((0,), (0,)), ((), ())), preferred_eleme...]
  transfers between devices with their start and end apart: 3 -> 0, of which waited for: 3 -> 0; matrix products, arithmetic and copies ran while one was open for 1% -> 0% of each run, Pallas kernels for 0% -> 0%
where the time goes in v2:
time: 59 us; the launch traced here: 58.8 us
  Pallas kernels  57.5 us (97%)
  between operations  1.29 us (2%)
    pallas_call x1, Pallas kernels, per_device(): pl.pallas_call(kernel, out_shape=shapes, in_specs=[hbm] * 6, out_specs=(a...  55.6 us
    pallas_call x1, Pallas kernels, per_device(): pl.pallas_call(hand_out, out_shape=shapes, in_specs=[vm] * 3, out_specs=(...  1.89 us

profile of v2, /device:TPU:1, one launch (start us, length us, event | category | flops | bytes accessed | tf_op | source)
XLA Modules:
  0.0 58.8 jit_solution(11544767367250145979)
XLA Ops:
  1.3 55.6 %shard_map.85 = (bf16[256,1024]{1,0:T(8,128)(2,1)}, f32[8,1024]{1,0:T(8,128)}, s32[1,8]{1,0:T(1,128)}) custom-call(bf16[256,1024]{1,0:T(8,128)(2,1)} %acts.1, f32[1,1024]{1,0:T(1,128)} %bitcast.5, bf16[8,1024]{1,0:T(8,128)(2,1)} %left.1, bf16[8,1024]{1,0:T(8,128)(2,1)} %right.1, s32[1,256]{1,0:T(1,128)} %bitcast.6, s32[1,1]{1,0:T(1,128)} %bitcast.4.counts), custom_call_target="tpu_custom_call" | custom-call | flops 805306368 | bytes 4194304 | tf_op jit(solution)/shard_map/pallas_call | solution.py:302
  56.9 1.9 %shard_map.86 = (bf16[256,1024]{1,0:T(8,128)(2,1)}, f32[8,1024]{1,0:T(8,128)}, s32[1,8]{1,0:T(1,128)}) custom-call(bf16[256,1024]{1,0:T(8,128)(2,1)} %get-tuple-element.9.erased, f32[8,1024]{1,0:T(8,128)} %get-tuple-element.10.scores, s32[1,8]{1,0:T(1,128)} %get-tuple-element.11.cnt), custom_call_target="tpu_custom_call" | custom-call | tf_op jit(solution)/shard_map/pallas_call | solution.py:359

commit v3 on v2

--- a/solution.py
+++ b/solution.py
@@ -20,8 +20,7 @@
 GROUPS = ((0, 2), (2, 2), (4, 2), (6, 2))
 TOK, D, RD = 256, 1024, 8
 T2, H, K2 = 512, 512, 128
-QN = 2
-QW = H // QN
+M = 24
 YB = T2 // NY
 VLIM = 63 << 20
 
@@ -29,10 +28,10 @@
 def kernel(
     acts, mean, left, right, labels, counts,
     out, scores, cnt,
-    meanv, labv, cntv, actv, cen, rg, lg, lo, lm, lab, pbuf, prx, cbuf, oh, er,
-    sxs, sxr, s0, txs, txr, szs, szr, tzs, tzr, fin,
+    meanv, labv, cntv, actv, cen, rg, lg, lo, lm, lab, labo, pbuf, prx, cbuf, oh, er,
+    sxs, sxr, s0, txs, txr, szs, szr, tzs, tzr, mh, rall, gy, gx, fin,
     loc, rzs, rzr, rxs, rxr, lzs, lzr, lxs, lxr, bzs, bzr, bxs, bxr, exs, exr,
-    pss, psr, css, csr, fcs, fcr, xxs, xxr, zzs, zzr,
+    pss, psr, css, csr, fcs, fcr, xxs, xxr, zzs, zzr, ggs, ggr,
 ):
     dp, y = lax.axis_index("dp"), lax.axis_index("tensor")
     c, x, z = lax.rem(dp, 2), lax.rem(dp // 2, NX), dp // (2 * NX)
@@ -112,27 +111,46 @@
         cp.wait()
     cen[mine, :] = (actv[mine, :].astype(F32) - meanv[...]).astype(BF16)
     slot_iota = lax.broadcasted_iota(I32, (1, TOK), 1)
-    lab[0, 0, 0] = jnp.where(slot_iota < cntv[...], labv[...], -1)
-
-    for g, (first, number) in enumerate(GROUPS):
-        fresh = max(first, 1)
-        got(rg.at[0, fresh : first + number], (rzr, g))
+    lab[0, 0, 0] = jnp.where(slot_iota < cntv[0], labv[...], -1)
+    send(lab.at[0, 0, 0], labo, (exs, 5), (exr, 5), other)
+
+    def right_x(g):
+        first, number = GROUPS[g]
+        got(rg.at[0, max(first, 1) : first + number], (rzr, g))
         zs = pl.ds(first, number)
-        along_x(lambda s: rg.at[0, zs], lambda t: rg.at[t, zs], (rxs, 0), lambda t: (rxr, t))
-
-    along_z(NEAR, lambda s: lab.at[0, 0, 0], lambda t: lab.at[0, 0, t], (bzs, 0), lambda t: (bzr, 0))
-    along_z(NEAR, lambda s: lg.at[0, 0], lambda t: lg.at[0, t], (lzs, 0), lambda t: (lzr, 0))
+        along_x(lambda s: rg.at[0, zs], lambda t: rg.at[t, zs], (rxs, 0), lambda t: (rxr, first // 4))
+
+    half, their_half = pl.ds(pl.multiple_of(c * H, H), H), pl.ds(pl.multiple_of(oc * H, H), H)
+    right_x(0)
+    right_x(1)
+    got(labo, (exr, 5))
+    tokens = jnp.concatenate([lab[0, 0, 0], labo[...]], axis=1)
+    for xs in range(NX):
+        for zs in range(NZ):
+            r = lax.broadcasted_iota(I32, (2 * RD, T2), 0)
+            owner = lax.rem(z + ZORD[zs], NZ) * NX + lax.rem(x + XORD[xs], NX)
+            at = (xs * NZ + zs) * 2 * RD
+            oh[at : at + 2 * RD, :] = (owner * (2 * RD) + r == tokens).astype(F32).astype(BF16)
     got(actv.at[theirs], (exr, 0))
     cen[theirs, :] = (actv[theirs, :].astype(F32) - meanv[...]).astype(BF16)
+    sums = jnp.dot(oh[...], actv[:, half], preferred_element_type=F32)
+    s0[...] = sums[:128]
+    txs[...] = jnp.sum(sums, axis=0, keepdims=True)
+    for s in range(1, NX):
+        sxs[s] = sums[s * 128 : (s + 1) * 128].astype(BF16)
+    right_x(2)
+    right_x(3)
+    along_x(lambda s: sxs.at[s], lambda t: sxr.at[t], (xxs, 0), lambda t: (xxr, 0))
+    along_x(lambda s: txs, lambda t: txr.at[t], (xxs, 1), lambda t: (xxr, 1))
+    along_z(NEAR, lambda s: lab.at[0, 0, 0], lambda t: lab.at[0, 0, t], (bzs, 0), lambda t: (bzr, 0))
 
     def block(s, turn=0):
         return pl.ds(pl.multiple_of(lax.rem(y + ZORD[s] + turn, NY) * YB, YB), YB)
 
     def chunk(k):
-        for xs in (2 * k, 2 * k + 1):
-            if xs:
-                got(rg.at[xs], (rxr, xs))
-        rmat = rg[2 * k : 2 * k + 2].astype(F32).reshape(K2, D).astype(BF16)
+        got(rg.at[1:NX, 4 * k : 4 * k + 4], (rxr, k))
+        rmat = rg[:, 4 * k : 4 * k + 4].astype(F32).reshape(K2, D).astype(BF16)
+        rall[k * K2 : (k + 1) * K2, :] = rmat
         part = lax.dot_general(cen[...], rmat, (((1,), (1,)), ((), ())), preferred_element_type=F32)
         pbuf[k] = part.astype(BF16)
         along_y(FAR, lambda s: pbuf.at[k, block(s)], lambda t: prx.at[k, t], (pss, k), lambda t: (psr, k))
@@ -156,22 +174,33 @@
             got(cbuf.at[0, k, block(s)], (csr, k * NY + s))
             across(k, s)
 
+    along_z(NEAR, lambda s: lg.at[0, 0], lambda t: lg.at[0, t], (lzs, 0), lambda t: (lzr, 0))
     chunk(0)
-    chunk(1)
     got(lab.at[0, 0, 1:NZ], (bzr, 0))
     along_x(lambda s: lab.at[0, 0], lambda t: lab.at[0, t], (bxs, 0), lambda t: (bxr, 0))
+    chunk(1)
     got(lg.at[0, 1:NZ], (lzr, 0))
     along_x(lambda s: lg.at[0], lambda t: lg.at[t], (lxs, 0), lambda t: (lxr, 0))
-
-    reduce(0)
-    reduce(1)
-
     got(lab.at[0, 1:NX], (bxr, 0))
     send(lab.at[0], lab.at[1], (exs, 1), (exr, 1), other)
-    got(lg.at[1:NX], (lxr, 0))
-    half, their_half = pl.ds(pl.multiple_of(c * H, H), H), pl.ds(pl.multiple_of(oc * H, H), H)
-    send(lg.at[:, :, :, their_half], lo, (exs, 2), (exr, 2), other)
-    lm[0:256, :] = lg[:, :, :, half].astype(F32).reshape(256, H).astype(BF16)
+
+    reduce(0)
+    total = s0[...]
+    got(sxr.at[1:NX], (xxr, 0))
+    for s in range(1, NX):
+        total = total + sxr[s].astype(F32)
+    for s in NEAR:
+        szs[s] = total[s * 2 * RD : (s + 1) * 2 * RD, :].astype(BF16)
+    mh[0, 0 : 2 * RD, :] = total[0 : 2 * RD]
+    along_z(FAR, lambda s: szs.at[s], lambda t: szr.at[t], (zzs, 0), lambda t: (zzr, 0))
+    total = txs[...]
+    got(txr.at[1:NX], (xxr, 1))
+    for s in range(1, NX):
+        total = total + txr[s]
+    tzs[...] = total
+    along_z(FAR, lambda s: tzs, lambda t: tzr.at[t], (zzs, 1), lambda t: (zzr, 1))
+    reduce(1)
+
     got(lab.at[1], (exr, 1))
     chip = z * NX + x
     own_class = chip * (2 * RD) + lax.broadcasted_iota(I32, (2 * RD, TOK), 0)
@@ -184,68 +213,66 @@
                 valid = valid + (row >= 0).astype(F32)
     own_counts = jnp.sum(hits, axis=1, keepdims=True)
     grand = jnp.sum(valid, axis=1, keepdims=True)
-    tokens = jnp.concatenate([lab[0, 0, 0], lab[1, 0, 0]], axis=1)
-    for xs in range(NX):
-        for zs in range(NZ):
-            r = lax.broadcasted_iota(I32, (2 * RD, T2), 0)
-            owner = lax.rem(z + ZORD[zs], NZ) * NX + lax.rem(x + XORD[xs], NX)
-            at = (xs * NZ + zs) * 2 * RD
-            oh[at : at + 2 * RD, :] = (owner * (2 * RD) + r == tokens).astype(F32).astype(BF16)
+    every = jnp.concatenate([own_counts, jnp.broadcast_to(grand, (M - 2 * RD, 1))], axis=0)
 
     gathered(0)
+    got(lg.at[1:NX], (lxr, 0))
+    send(lg.at[:, :, :, their_half], lo, (exs, 2), (exr, 2), other)
+    for k in range(2):
+        lm[k * K2 : (k + 1) * K2, :] = lg[:, 4 * k : 4 * k + 4, :, half].astype(F32).reshape(K2, H).astype(BF16)
+
+    got(szr.at[1:NZ], (zzr, 0))
+    got(tzr.at[1:NZ], (zzr, 1))
+    class_sums, total = mh[0, 0 : 2 * RD, :], tzs[...]
+    for s in range(1, NZ):
+        class_sums = class_sums + szr[s].astype(F32)
+        total = total + tzr[s]
+    mh[0, 0 : 2 * RD, :] = class_sums
+    mh[0, 2 * RD : M, :] = jnp.broadcast_to(total, (M - 2 * RD, H))
+    send(mh.at[0], mh.at[1], (exs, 6), (exr, 6), other)
+    gathered(1)
+
+    def twice(a, b, dims):
+        high = a.astype(BF16)
+        low = (a - high.astype(F32)).astype(BF16)
+        dims = (dims, ((), ()))
+        return lax.dot_general(high, b, dims, preferred_element_type=F32) + lax.dot_general(
+            low, b, dims, preferred_element_type=F32
+        )
+
+    got(mh.at[1], (exr, 6))
+    gsum = twice(mh[0] - every * meanv[:, half], rall[:, half], ((1,), (1,)))
+    gsum = gsum + twice(mh[1] - every * meanv[:, their_half], rall[:, their_half], ((1,), (1,)))
+    gy[0] = gsum
+    along_y(FAR, lambda s: gy.at[0], lambda t: gy.at[t], (ggs, 0), lambda t: (ggr, 0))
+
     got(lo, (exr, 2))
-    lm[256:512, :] = lo[...].astype(F32).reshape(256, H).astype(BF16)
-    gathered(1)
+    for k in range(2, 4):
+        lm[k * K2 : (k + 1) * K2, :] = lo[:, 4 * k - 8 : 4 * k - 4].astype(F32).reshape(K2, H).astype(BF16)
     for k in range(2):
         got(cbuf.at[1, k], (fcr, k))
 
     coords = jnp.concatenate([cbuf[0, 0], cbuf[0, 1], cbuf[1, 0], cbuf[1, 1]], axis=1)
-    for q in range(QN):
-        cols = slice(q * QW, (q + 1) * QW)
-        corr = jnp.dot(coords, lm[:, cols], preferred_element_type=F32)
-        acols = pl.ds(pl.multiple_of(c * H + q * QW, QW), QW)
-        er[:, cols] = (actv[:, acols].astype(F32) - corr).astype(BF16)
-        sums = jnp.dot(oh[...], er[:, cols], preferred_element_type=F32)
-        s0[:, cols] = sums[:128]
-        txs[:, cols] = jnp.sum(sums, axis=0, keepdims=True)
-        for s in range(1, NX):
-            sxs[q, s] = sums[s * 128 : (s + 1) * 128].astype(BF16)
-        along_x(lambda s: sxs.at[q, s], lambda t: sxr.at[q, t], (xxs, q), lambda t: (xxr, q))
-    along_x(lambda s: txs, lambda t: txr.at[t], (xxs, QN), lambda t: (xxr, QN))
+    for rows in (theirs, mine):
+        at = rows.start
+        corr = jnp.dot(coords[at : at + TOK], lm[...], preferred_element_type=F32)
+        er[rows, :] = (actv[rows, half].astype(F32) - corr).astype(BF16)
+        if at:
+            send(er.at[theirs], out.at[:, half], (exs, 3), (exr, 3), other)
     keep = pltpu.make_async_copy(er.at[mine], out.at[:, half], loc.at[6])
     keep.start()
-    send(er.at[theirs], out.at[:, half], (exs, 3), (exr, 3), other)
-
-    for q in range(QN):
-        cols = slice(q * QW, (q + 1) * QW)
-        total = s0[:, cols]
-        got(sxr.at[q, 1:NX], (xxr, q))
-        for s in range(1, NX):
-            total = total + sxr[q, s].astype(F32)
-        for s in NEAR:
-            szs[q, s] = total[s * 2 * RD : (s + 1) * 2 * RD, :].astype(BF16)
-        s0[0 : 2 * RD, cols] = total[0 : 2 * RD]
-        along_z(FAR, lambda s: szs.at[q, s], lambda t: szr.at[q, t], (zzs, q), lambda t: (zzr, q))
-    total = txs[...]
-    got(txr.at[1:NX], (xxr, QN))
-    for s in range(1, NX):
-        total = total + txr[s]
-    tzs[...] = total
-    along_z(FAR, lambda s: tzs, lambda t: tzr.at[t], (zzs, QN), lambda t: (zzr, QN))
-
+
+    got(gy.at[1:NY], (ggr, 0))
+    for s in range(1, NY):
+        gsum = gsum + gy[s]
+    gx[0] = gsum
+    send(gx.at[0], gx.at[1], (exs, 7), (exr, 7), other)
+    result = mh[0] - twice(gsum, lm[0:256, :], ((1,), (0,)))
+    got(gx.at[1], (exr, 7))
+    result = result - twice(gx[1], lm[256:512, :], ((1,), (0,)))
     scale = 1.0 / jnp.sqrt(jnp.maximum(own_counts, 1.0))
-    got(szr.at[0, 1:NZ], (zzr, 0))
-    got(szr.at[1, 1:NZ], (zzr, 1))
-    got(tzr.at[1:NZ], (zzr, QN))
-    for s in range(1, NZ):
-        total = total + tzr[s]
-    feature_mean = total / grand
-    for q in range(QN):
-        cols = slice(q * QW, (q + 1) * QW)
-        class_sums = s0[0 : 2 * RD, cols]
-        for s in range(1, NZ):
-            class_sums = class_sums + szr[q, s].astype(F32)
-        fin[:, cols] = (class_sums - own_counts * feature_mean[:, cols]) * scale
+    feature_mean = result[2 * RD : 2 * RD + 1, :] / grand
+    fin[...] = (result[0 : 2 * RD] - own_counts * feature_mean) * scale
     own_fin = fin.at[pl.ds(pl.multiple_of(c * RD, RD), RD)]
     send(fin.at[pl.ds(pl.multiple_of(oc * RD, RD), RD)], scores.at[:, half], (exs, 4), (exr, 4), other)
     put = pltpu.make_async_copy(own_fin, scores.at[:, half], loc.at[7])
@@ -269,11 +296,14 @@
         gone(prx.at[k, 1:NY], (pss, k))
         gone(prx.at[k, 1:NY], (css, k))
         gone(cbuf.at[0, k], (fcs, k))
-    for q in range(QN):
-        gone(sxr.at[q, 1:NX], (xxs, q))
-        gone(szr.at[q, 1:NZ], (zzs, q))
-    gone(txr.at[1:NX], (xxs, QN))
-    gone(tzr.at[1:NZ], (zzs, QN))
+    gone(sxr.at[1:NX], (xxs, 0))
+    gone(szr.at[1:NZ], (zzs, 0))
+    gone(txr.at[1:NX], (xxs, 1))
+    gone(tzr.at[1:NZ], (zzs, 1))
+    gone(gy.at[1:NY], (ggs, 0))
+    gone(labo, (exs, 5))
+    gone(mh.at[0], (exs, 6))
+    gone(gx.at[0], (exs, 7))
     gone(own_fin, (exs, 4))
     got(er.at[theirs], (exr, 3))
     put.wait()
@@ -307,7 +337,7 @@
         scratch_shapes=[
             pltpu.VMEM((1, D), F32),
             pltpu.VMEM((1, TOK), I32),
-            pltpu.VMEM((1, 1), I32),
+            pltpu.SMEM((1,), I32),
             pltpu.VMEM((T2, D), BF16),
             pltpu.VMEM((T2, D), BF16),
             pltpu.VMEM((NX, NZ, RD, D), BF16),
@@ -315,34 +345,40 @@
             pltpu.VMEM((NX, NZ, RD, H), BF16),
             pltpu.VMEM((C, H), BF16),
             pltpu.VMEM((2, NX, NZ, 1, TOK), I32),
+            pltpu.VMEM((1, TOK), I32),
             pltpu.VMEM((2, T2, K2), BF16),
             pltpu.VMEM((2, NY, YB, K2), BF16),
             pltpu.VMEM((2, 2, T2, K2), BF16),
             pltpu.VMEM((C, T2), BF16),
             pltpu.VMEM((T2, H), BF16),
-            pltpu.VMEM((QN, NX, 128, QW), BF16),
-            pltpu.VMEM((QN, NX, 128, QW), BF16),
+            pltpu.VMEM((NX, 128, H), BF16),
+            pltpu.VMEM((NX, 128, H), BF16),
             pltpu.VMEM((128, H), F32),
             pltpu.VMEM((1, H), F32),
             pltpu.VMEM((NX, 1, H), F32),
-            pltpu.VMEM((QN, NZ, 2 * RD, QW), BF16),
-            pltpu.VMEM((QN, NZ, 2 * RD, QW), BF16),
+            pltpu.VMEM((NZ, 2 * RD, H), BF16),
+            pltpu.VMEM((NZ, 2 * RD, H), BF16),
             pltpu.VMEM((1, H), F32),
             pltpu.VMEM((NZ, 1, H), F32),
+            pltpu.VMEM((2, M, H), F32),
+            pltpu.VMEM((256, D), BF16),
+            pltpu.VMEM((NY, M, 256), F32),
+            pltpu.VMEM((2, M, 256), F32),
             pltpu.VMEM((2 * RD, H), F32),
             dma((8,)),
             dma((1,)), dma((ng,)),
-            dma((1,)), dma((NX,)),
+            dma((1,)), dma((2,)),
             dma((1,)), dma((1,)),
             dma((1,)), dma((1,)),
             dma((1,)), dma((1,)),
             dma((1,)), dma((1,)),
-            dma((5,)), dma((5,)),
+            dma((8,)), dma((8,)),
             dma((2,)), dma((2,)),
             dma((2,)), dma((2 * NY,)),
             dma((2,)), dma((2,)),
-            dma((QN + 1,)), dma((QN + 1,)),
-            dma((QN + 1,)), dma((QN + 1,)),
+            dma((2,)), dma((2,)),
+            dma((2,)), dma((2,)),
+            dma((1,)), dma((1,)),
         ],
         compiler_params=pltpu.CompilerParams(
             collective_id=0, has_side_effects=True, vmem_limit_bytes=VLIM
@@ -354,7 +390,7 @@
         left_factor,
         right_factor,
         labels.reshape(1, TOK),
-        counts.reshape(1, 1),
+        counts,
     )
     erased, scores, cnt = pl.pallas_call(
         hand_out,

time: 59 us -> 54.9 us (0.931)
  Pallas kernels: 57.5 us -> 53.4 us
    pallas_call x1, Pallas kernels: 55.6 us -> 51.5 us  [per_device(): pl.pallas_call(kernel, out_shape=shapes, in_specs=[hbm] * 6, out_specs=(a...]
where the time goes in v3:
time: 54.9 us; the launch traced here: 54.7 us
  Pallas kernels  53.4 us (97%)
  between operations  1.29 us (2%)
    pallas_call x1, Pallas kernels, per_device(): pl.pallas_call(kernel, out_shape=shapes, in_specs=[hbm] * 6, out_specs=(a...  51.5 us
    pallas_call x1, Pallas kernels, per_device(): pl.pallas_call(hand_out, out_shape=shapes, in_specs=[vm] * 3, out_specs=(...  1.89 us

profile of v3, /device:TPU:1, one launch (start us, length us, event | category | flops | bytes accessed | tf_op | source)
XLA Modules:
  0.0 54.7 jit_solution(9396548342726181238)
XLA Ops:
  1.3 51.5 %shard_map.85 = (bf16[256,1024]{1,0:T(8,128)(2,1)}, f32[8,1024]{1,0:T(8,128)}, s32[1,8]{1,0:T(1,128)}) custom-call(bf16[256,1024]{1,0:T(8,128)(2,1)} %acts.1, f32[1,1024]{1,0:T(1,128)} %bitcast.3, bf16[8,1024]{1,0:T(8,128)(2,1)} %left.1, bf16[8,1024]{1,0:T(8,128)(2,1)} %right.1, s32[1,256]{1,0:T(1,128)} %bitcast.4, s32[1]{0:T(128)S(6)} %copy.9.counts), custom_call_target="tpu_custom_call" | custom-call | flops 805306368 | bytes 4194304 | tf_op jit(solution)/shard_map/pallas_call | solution.py:332
  52.8 1.9 %shard_map.86 = (bf16[256,1024]{1,0:T(8,128)(2,1)}, f32[8,1024]{1,0:T(8,128)}, s32[1,8]{1,0:T(1,128)}) custom-call(bf16[256,1024]{1,0:T(8,128)(2,1)} %get-tuple-element.9.erased, f32[8,1024]{1,0:T(8,128)} %get-tuple-element.10.scores, s32[1,8]{1,0:T(1,128)} %get-tuple-element.11.cnt), custom_call_target="tpu_custom_call" | custom-call | tf_op jit(solution)/shard_map/pallas_call | solution.py:395

commit v4 on v3

--- a/solution.py
+++ b/solution.py
@@ -20,16 +20,17 @@
 GROUPS = ((0, 2), (2, 2), (4, 2), (6, 2))
 TOK, D, RD = 256, 1024, 8
 T2, H, K2 = 512, 512, 128
-M = 24
+M = 2 * RD
 YB = T2 // NY
 VLIM = 63 << 20
+PIECES = 4
 
 
 def kernel(
     acts, mean, left, right, labels, counts,
     out, scores, cnt,
     meanv, labv, cntv, actv, cen, rg, lg, lo, lm, lab, labo, pbuf, prx, cbuf, oh, er,
-    sxs, sxr, s0, txs, txr, szs, szr, tzs, tzr, mh, rall, gy, gx, fin,
+    sxs, sxr, s0, txs, txr, szs, szr, tzs, tzr, mh, rall, gy, gx, cnts,
     loc, rzs, rzr, rxs, rxr, lzs, lzr, lxs, lxr, bzs, bzr, bxs, bxr, exs, exr,
     pss, psr, css, csr, fcs, fcr, xxs, xxr, zzs, zzr, ggs, ggr,
 ):
@@ -139,9 +140,9 @@
     for s in range(1, NX):
         sxs[s] = sums[s * 128 : (s + 1) * 128].astype(BF16)
     right_x(2)
-    right_x(3)
     along_x(lambda s: sxs.at[s], lambda t: sxr.at[t], (xxs, 0), lambda t: (xxr, 0))
     along_x(lambda s: txs, lambda t: txr.at[t], (xxs, 1), lambda t: (xxr, 1))
+    right_x(3)
     along_z(NEAR, lambda s: lab.at[0, 0, 0], lambda t: lab.at[0, 0, t], (bzs, 0), lambda t: (bzr, 0))
 
     def block(s, turn=0):
@@ -184,7 +185,6 @@
     got(lab.at[0, 1:NX], (bxr, 0))
     send(lab.at[0], lab.at[1], (exs, 1), (exr, 1), other)
 
-    reduce(0)
     total = s0[...]
     got(sxr.at[1:NX], (xxr, 0))
     for s in range(1, NX):
@@ -199,6 +199,7 @@
         total = total + txr[s]
     tzs[...] = total
     along_z(FAR, lambda s: tzs, lambda t: tzr.at[t], (zzs, 1), lambda t: (zzr, 1))
+    reduce(0)
     reduce(1)
 
     got(lab.at[1], (exr, 1))
@@ -213,49 +214,43 @@
                 valid = valid + (row >= 0).astype(F32)
     own_counts = jnp.sum(hits, axis=1, keepdims=True)
     grand = jnp.sum(valid, axis=1, keepdims=True)
-    every = jnp.concatenate([own_counts, jnp.broadcast_to(grand, (M - 2 * RD, 1))], axis=0)
-
-    gathered(0)
-    got(lg.at[1:NX], (lxr, 0))
-    send(lg.at[:, :, :, their_half], lo, (exs, 2), (exr, 2), other)
-    for k in range(2):
-        lm[k * K2 : (k + 1) * K2, :] = lg[:, 4 * k : 4 * k + 4, :, half].astype(F32).reshape(K2, H).astype(BF16)
 
     got(szr.at[1:NZ], (zzr, 0))
     got(tzr.at[1:NZ], (zzr, 1))
-    class_sums, total = mh[0, 0 : 2 * RD, :], tzs[...]
+    class_sums, total = mh[0], tzs[...]
     for s in range(1, NZ):
         class_sums = class_sums + szr[s].astype(F32)
         total = total + tzr[s]
-    mh[0, 0 : 2 * RD, :] = class_sums
-    mh[0, 2 * RD : M, :] = jnp.broadcast_to(total, (M - 2 * RD, H))
+    mh[0] = class_sums - own_counts * (total / grand)
     send(mh.at[0], mh.at[1], (exs, 6), (exr, 6), other)
+    gathered(0)
+
+    def twice(a, b, dims):
+        high = a.astype(BF16).astype(F32)
+        terms = jnp.concatenate([high, a - high], axis=0).astype(BF16)
+        both = lax.dot_general(terms, b, (dims, ((), ())), preferred_element_type=F32)
+        return both[: a.shape[0]] + both[a.shape[0] :]
+
+    got(mh.at[1], (exr, 6))
+    gsum = twice(mh[0], rall[:, half], ((1,), (1,))) + twice(mh[1], rall[:, their_half], ((1,), (1,)))
+    gy[0] = gsum.astype(BF16)
+    along_y(FAR, lambda s: gy.at[0], lambda t: gy.at[t], (ggs, 0), lambda t: (ggr, 0))
+
+    got(lg.at[1:NX], (lxr, 0))
+    send(lg, lo, (exs, 2), (exr, 2), other)
+    for k in range(2):
+        lm[k * K2 : (k + 1) * K2, :] = lg[:, 4 * k : 4 * k + 4].astype(F32).reshape(K2, D).astype(BF16)
     gathered(1)
-
-    def twice(a, b, dims):
-        high = a.astype(BF16)
-        low = (a - high.astype(F32)).astype(BF16)
-        dims = (dims, ((), ()))
-        return lax.dot_general(high, b, dims, preferred_element_type=F32) + lax.dot_general(
-            low, b, dims, preferred_element_type=F32
-        )
-
-    got(mh.at[1], (exr, 6))
-    gsum = twice(mh[0] - every * meanv[:, half], rall[:, half], ((1,), (1,)))
-    gsum = gsum + twice(mh[1] - every * meanv[:, their_half], rall[:, their_half], ((1,), (1,)))
-    gy[0] = gsum
-    along_y(FAR, lambda s: gy.at[0], lambda t: gy.at[t], (ggs, 0), lambda t: (ggr, 0))
-
     got(lo, (exr, 2))
     for k in range(2, 4):
-        lm[k * K2 : (k + 1) * K2, :] = lo[:, 4 * k - 8 : 4 * k - 4].astype(F32).reshape(K2, H).astype(BF16)
+        lm[k * K2 : (k + 1) * K2, :] = lo[:, 4 * k - 8 : 4 * k - 4].astype(F32).reshape(K2, D).astype(BF16)
     for k in range(2):
         got(cbuf.at[1, k], (fcr, k))
 
     coords = jnp.concatenate([cbuf[0, 0], cbuf[0, 1], cbuf[1, 0], cbuf[1, 1]], axis=1)
     for rows in (theirs, mine):
         at = rows.start
-        corr = jnp.dot(coords[at : at + TOK], lm[...], preferred_element_type=F32)
+        corr = jnp.dot(coords[at : at + TOK], lm[:, half], preferred_element_type=F32)
         er[rows, :] = (actv[rows, half].astype(F32) - corr).astype(BF16)
         if at:
             send(er.at[theirs], out.at[:, half], (exs, 3), (exr, 3), other)
@@ -264,22 +259,22 @@
 
     got(gy.at[1:NY], (ggr, 0))
     for s in range(1, NY):
-        gsum = gsum + gy[s]
+        gsum = gsum + gy[s].astype(F32)
     gx[0] = gsum
-    send(gx.at[0], gx.at[1], (exs, 7), (exr, 7), other)
-    result = mh[0] - twice(gsum, lm[0:256, :], ((1,), (0,)))
-    got(gx.at[1], (exr, 7))
-    result = result - twice(gx[1], lm[256:512, :], ((1,), (0,)))
+    ours, others = pl.ds(pl.multiple_of(c * RD, RD), RD), pl.ds(pl.multiple_of(oc * RD, RD), RD)
+    send(gx.at[0, others], gx.at[1, others], (exs, 7), (exr, 7), other)
+    cnts[...] = jnp.broadcast_to(own_counts, (M, 128))
+    own_counts = cnts[ours, 0:1]
+    lane = lax.broadcasted_iota(I32, (RD, RD), 1)
+    row = lax.broadcasted_iota(I32, (RD, RD), 0)
+    cnt[...] = jnp.sum(jnp.where(lane == row, own_counts, 0.0), axis=0, keepdims=True).astype(I32)
     scale = 1.0 / jnp.sqrt(jnp.maximum(own_counts, 1.0))
-    feature_mean = result[2 * RD : 2 * RD + 1, :] / grand
-    fin[...] = (result[0 : 2 * RD] - own_counts * feature_mean) * scale
-    own_fin = fin.at[pl.ds(pl.multiple_of(c * RD, RD), RD)]
-    send(fin.at[pl.ds(pl.multiple_of(oc * RD, RD), RD)], scores.at[:, half], (exs, 4), (exr, 4), other)
-    put = pltpu.make_async_copy(own_fin, scores.at[:, half], loc.at[7])
-    put.start()
-    lane = lax.broadcasted_iota(I32, (2 * RD, RD), 1)
-    row = lax.broadcasted_iota(I32, (2 * RD, RD), 0)
-    cnt[...] = jnp.sum(jnp.where(lane + c * RD == row, own_counts, 0.0), axis=0, keepdims=True).astype(I32)
+    got(gx.at[1, ours], (exr, 7))
+    coords = jnp.concatenate([gx[0, ours, :], gx[1, ours, :]], axis=1)
+    moved = twice(coords, lm[...], ((1,), (0,)))
+    scores[...] = moved * -scale
+    for k, cols in enumerate((half, their_half)):
+        scores[:, cols] += mh[k, ours, :] * scale
 
     keep.wait()
     gone(rg.at[0, 1:NZ], (rzs, 0))
@@ -303,19 +298,23 @@
     gone(gy.at[1:NY], (ggs, 0))
     gone(labo, (exs, 5))
     gone(mh.at[0], (exs, 6))
-    gone(gx.at[0], (exs, 7))
-    gone(own_fin, (exs, 4))
+    gone(gx.at[0, others], (exs, 7))
     got(er.at[theirs], (exr, 3))
-    put.wait()
-    got(own_fin, (exr, 4))
-
-
-def hand_out(erased, scores, cnt, erased_out, scores_out, cnt_out, sems):
-    pairs = ((erased, erased_out), (scores, scores_out), (cnt, cnt_out))
-    copies = [pltpu.make_async_copy(a, b, sems.at[i]) for i, (a, b) in enumerate(pairs)]
-    for cp in copies:
+
+
+def hand_out(erased, scores, cnt, erased_out, scores_out, cnt_out, erased_v, scores_v, cnt_v, sems):
+    rows = TOK // PIECES
+    parts = [pl.ds(i * rows, rows) for i in range(PIECES)]
+    trips = [(erased.at[p], erased_v.at[p], erased_out.at[p]) for p in parts]
+    trips += [(scores, scores_v, scores_out), (cnt, cnt_v, cnt_out)]
+    ins = [pltpu.make_async_copy(a, v, sems.at[0, i]) for i, (a, v, _) in enumerate(trips)]
+    outs = [pltpu.make_async_copy(v, b, sems.at[1, i]) for i, (_, v, b) in enumerate(trips)]
+    for cp in ins:
         cp.start()
-    for cp in copies:
+    for load, store in zip(ins, outs):
+        load.wait()
+        store.start()
+    for cp in outs:
         cp.wait()
 
 
@@ -333,7 +332,7 @@
         kernel,
         out_shape=shapes,
         in_specs=[hbm] * 6,
-        out_specs=(anywhere, anywhere, vm),
+        out_specs=(anywhere, vm, vm),
         scratch_shapes=[
             pltpu.VMEM((1, D), F32),
             pltpu.VMEM((1, TOK), I32),
@@ -342,8 +341,8 @@
             pltpu.VMEM((T2, D), BF16),
             pltpu.VMEM((NX, NZ, RD, D), BF16),
             pltpu.VMEM((NX, NZ, RD, D), BF16),
-            pltpu.VMEM((NX, NZ, RD, H), BF16),
-            pltpu.VMEM((C, H), BF16),
+            pltpu.VMEM((NX, NZ, RD, D), BF16),
+            pltpu.VMEM((C, D), BF16),
             pltpu.VMEM((2, NX, NZ, 1, TOK), I32),
             pltpu.VMEM((1, TOK), I32),
             pltpu.VMEM((2, T2, K2), BF16),
@@ -362,9 +361,9 @@
             pltpu.VMEM((NZ, 1, H), F32),
             pltpu.VMEM((2, M, H), F32),
             pltpu.VMEM((256, D), BF16),
-            pltpu.VMEM((NY, M, 256), F32),
+            pltpu.VMEM((NY, M, 256), BF16),
             pltpu.VMEM((2, M, 256), F32),
-            pltpu.VMEM((2 * RD, H), F32),
+            pltpu.VMEM((M, 128), F32),
             dma((8,)),
             dma((1,)), dma((ng,)),
             dma((1,)), dma((2,)),
@@ -395,9 +394,10 @@
     erased, scores, cnt = pl.pallas_call(
         hand_out,
         out_shape=shapes,
-        in_specs=[vm] * 3,
+        in_specs=[hbm] * 3,
         out_specs=(hbm,) * 3,
-        scratch_shapes=[dma((3,))],
+        scratch_shapes=[pltpu.VMEM(v.shape, v.dtype) for v in shapes] + [dma((2, PIECES + 2))],
+        compiler_params=pltpu.CompilerParams(vmem_limit_bytes=VLIM),
     )(*results)
     return erased, scores, cnt.reshape(RD)
 

time: 54.9 us -> 51.1 us (0.931)
  Pallas kernels: 53.4 us -> 49.6 us
    pallas_call x1, Pallas kernels: 51.5 us -> 47.7 us  [per_device(): pl.pallas_call(kernel, out_shape=shapes, in_specs=[hbm] * 6, out_specs=(a...]
where the time goes in v4:
time: 51.1 us; the launch traced here: 50.9 us
  Pallas kernels  49.6 us (97%)
  between operations  1.29 us (3%)
    pallas_call x1, Pallas kernels, per_device(): pl.pallas_call(kernel, out_shape=shapes, in_specs=[hbm] * 6, out_specs=(a...  47.7 us
    pallas_call x1, Pallas kernels, per_device(): pl.pallas_call(hand_out, out_shape=shapes, in_specs=[hbm] * 3, out_specs=...  1.86 us

profile of v4, /device:TPU:1, one launch (start us, length us, event | category | flops | bytes accessed | tf_op | source)
XLA Modules:
  0.0 50.9 jit_solution(4327314900482803958)
XLA Ops:
  1.3 47.7 %shard_map.85 = (bf16[256,1024]{1,0:T(8,128)(2,1)}, f32[8,1024]{1,0:T(8,128)}, s32[1,8]{1,0:T(1,128)}) custom-call(bf16[256,1024]{1,0:T(8,128)(2,1)} %acts.1, f32[1,1024]{1,0:T(1,128)} %bitcast.3, bf16[8,1024]{1,0:T(8,128)(2,1)} %left.1, bf16[8,1024]{1,0:T(8,128)(2,1)} %right.1, s32[1,256]{1,0:T(1,128)} %bitcast.4, s32[1]{0:T(128)S(6)} %copy.9.counts), custom_call_target="tpu_custom_call" | custom-call | flops 805306368 | bytes 4194304 | tf_op jit(solution)/shard_map/pallas_call | solution.py:331
  49.0 1.9 %shard_map.86 = (bf16[256,1024]{1,0:T(8,128)(2,1)}, f32[8,1024]{1,0:T(8,128)}, s32[1,8]{1,0:T(1,128)}) custom-call(bf16[256,1024]{1,0:T(8,128)(2,1)} %get-tuple-element.9.erased, f32[8,1024]{1,0:T(8,128)} %get-tuple-element.10.scores, s32[1,8]{1,0:T(1,128)} %get-tuple-element.11.cnt), custom_call_target="tpu_custom_call" | custom-call | tf_op jit(solution)/shard_map/pallas_call | solution.py:394

commit v5 on v4

--- a/solution.py
+++ b/solution.py
@@ -21,6 +21,7 @@
 TOK, D, RD = 256, 1024, 8
 T2, H, K2 = 512, 512, 128
 M = 2 * RD
+XW, ZW = 384, 128
 YB = T2 // NY
 VLIM = 63 << 20
 PIECES = 4
@@ -29,10 +30,10 @@
 def kernel(
     acts, mean, left, right, labels, counts,
     out, scores, cnt,
-    meanv, labv, cntv, actv, cen, rg, lg, lo, lm, lab, labo, pbuf, prx, cbuf, oh, er,
-    sxs, sxr, s0, txs, txr, szs, szr, tzs, tzr, mh, rall, gy, gx, cnts,
+    meanv, labv, cntv, actv, cen, rg, lg, lo, lm, lab, labo, pbuf, prx, obuf, cbuf, oh, er,
+    sxs, sxr, s0, txs, txr, szs, szr, tzs, tzr, fzs, fzr, f0, fxs, fxr, mh, rall, gy, gx, cnts,
     loc, rzs, rzr, rxs, rxr, lzs, lzr, lxs, lxr, bzs, bzr, bxs, bxr, exs, exr,
-    pss, psr, css, csr, fcs, fcr, xxs, xxr, zzs, zzr, ggs, ggr,
+    pss, psr, css, csr, xxs, xxr, zzs, zzr, ffs, ffr, ggs, ggr,
 ):
     dp, y = lax.axis_index("dp"), lax.axis_index("tensor")
     c, x, z = lax.rem(dp, 2), lax.rem(dp // 2, NX), dp // (2 * NX)
@@ -97,7 +98,7 @@
         cp.start()
 
     barrier = pltpu.get_barrier_semaphore()
-    peers = [dev(dz=ZORD[s]) for s in FAR] + [dev(dy=ZORD[s]) for s in FAR]
+    peers = [dev(dz=ZORD[s]) for s in FAR] + [dev(dy=ZORD[s], core=k) for s in FAR for k in (c, oc)]
     peers += [dev(dx=d) for d in (2, 1, 3)] + [other]
     for p in peers:
         pl.semaphore_signal(barrier, inc=1, device_id=p, device_id_type=MESH)
@@ -135,18 +136,27 @@
     got(actv.at[theirs], (exr, 0))
     cen[theirs, :] = (actv[theirs, :].astype(F32) - meanv[...]).astype(BF16)
     sums = jnp.dot(oh[...], actv[:, half], preferred_element_type=F32)
-    s0[...] = sums[:128]
+    for zs in range(NZ):
+        for xs in range(NX):
+            at = (xs * NZ + zs) * M
+            part = sums[at : at + M, XW:]
+            if zs:
+                fzs[zs, xs * M : (xs + 1) * M, :] = part.astype(BF16)
+            else:
+                f0[xs * M : (xs + 1) * M, :] = part
+    along_z(NEAR, lambda s: fzs.at[s], lambda t: fzr.at[t], (ffs, 0), lambda t: (ffr, 0))
+    s0[...] = sums[:128, :XW]
     txs[...] = jnp.sum(sums, axis=0, keepdims=True)
     for s in range(1, NX):
-        sxs[s] = sums[s * 128 : (s + 1) * 128].astype(BF16)
-    right_x(2)
+        sxs[s] = sums[s * 128 : (s + 1) * 128, :XW].astype(BF16)
     along_x(lambda s: sxs.at[s], lambda t: sxr.at[t], (xxs, 0), lambda t: (xxr, 0))
     along_x(lambda s: txs, lambda t: txr.at[t], (xxs, 1), lambda t: (xxr, 1))
+    right_x(2)
     right_x(3)
     along_z(NEAR, lambda s: lab.at[0, 0, 0], lambda t: lab.at[0, 0, t], (bzs, 0), lambda t: (bzr, 0))
 
-    def block(s, turn=0):
-        return pl.ds(pl.multiple_of(lax.rem(y + ZORD[s] + turn, NY) * YB, YB), YB)
+    def block(s):
+        return pl.ds(pl.multiple_of(lax.rem(y + ZORD[s], NY) * YB, YB), YB)
 
     def chunk(k):
         got(rg.at[1:NX, 4 * k : 4 * k + 4], (rxr, k))
@@ -156,24 +166,35 @@
         pbuf[k] = part.astype(BF16)
         along_y(FAR, lambda s: pbuf.at[k, block(s)], lambda t: prx.at[k, t], (pss, k), lambda t: (psr, k))
 
-    def across(k, s):
-        ref, there = cbuf.at[0, k, block(s)], cbuf.at[1, k, block(s, NY // 2)]
-        send(ref, there, (fcs, k), (fcr, k), other)
+    near_half = y < NY // 2
+    taker = lax.rem(c + y // (NY // 2), 2)
 
     def reduce(k):
         total = pbuf[k, block(0), :].astype(F32)
         got(prx.at[k, 1:NY], (psr, k))
         for s in range(1, NY):
             total = total + prx[k, s].astype(F32)
-        own = cbuf.at[0, k, block(0)]
-        own[...] = total.astype(BF16)
-        along_y(FAR, lambda s: own, lambda t: own, (css, k), lambda t: (csr, k * NY + t))
-        across(k, 0)
+        obuf[k] = total.astype(BF16)
+        there = cbuf.at[k, block(0)]
+        for s in FAR:
+            send(obuf.at[k], there, (css, k), (csr, k), dev(dy=ZORD[s], core=taker))
+
+        @pl.when(near_half)
+        def _():
+            there[...] = obuf[k]
+
+        @pl.when(jnp.logical_not(near_half))
+        def _():
+            send(obuf.at[k], there, (css, k), (csr, k), other)
 
     def gathered(k):
-        for s in range(1, NY):
-            got(cbuf.at[0, k, block(s)], (csr, k * NY + s))
-            across(k, s)
+        @pl.when(near_half)
+        def _():
+            got(cbuf.at[k, 0 : T2 - YB], (csr, k))
+
+        @pl.when(jnp.logical_not(near_half))
+        def _():
+            got(cbuf.at[k], (csr, k))
 
     along_z(NEAR, lambda s: lg.at[0, 0], lambda t: lg.at[0, t], (lzs, 0), lambda t: (lzr, 0))
     chunk(0)
@@ -191,7 +212,7 @@
         total = total + sxr[s].astype(F32)
     for s in NEAR:
         szs[s] = total[s * 2 * RD : (s + 1) * 2 * RD, :].astype(BF16)
-    mh[0, 0 : 2 * RD, :] = total[0 : 2 * RD]
+    mh[0, :, 0:XW] = total[0:M]
     along_z(FAR, lambda s: szs.at[s], lambda t: szr.at[t], (zzs, 0), lambda t: (zzr, 0))
     total = txs[...]
     got(txr.at[1:NX], (xxr, 1))
@@ -199,6 +220,14 @@
         total = total + txr[s]
     tzs[...] = total
     along_z(FAR, lambda s: tzs, lambda t: tzr.at[t], (zzs, 1), lambda t: (zzr, 1))
+    total = f0[...]
+    got(fzr.at[1:NZ], (ffr, 0))
+    for s in range(1, NZ):
+        total = total + fzr[s].astype(F32)
+    mh[0, :, XW:] = total[0:M]
+    for s in range(1, NX):
+        fxs[s] = total[s * M : (s + 1) * M, :].astype(BF16)
+    along_x(lambda s: fxs.at[s], lambda t: fxr.at[t], (ffs, 1), lambda t: (ffr, 1))
     reduce(0)
     reduce(1)
 
@@ -215,15 +244,23 @@
     own_counts = jnp.sum(hits, axis=1, keepdims=True)
     grand = jnp.sum(valid, axis=1, keepdims=True)
 
+    got(lg.at[1:NX], (lxr, 0))
+    send(lg, lo, (exs, 2), (exr, 2), other)
+    for k in range(2):
+        lm[k * K2 : (k + 1) * K2, :] = lg[:, 4 * k : 4 * k + 4].astype(F32).reshape(K2, D).astype(BF16)
     got(szr.at[1:NZ], (zzr, 0))
     got(tzr.at[1:NZ], (zzr, 1))
-    class_sums, total = mh[0], tzs[...]
+    first_sums, other_sums, total = mh[0, :, 0:XW], mh[0, :, XW:], tzs[...]
     for s in range(1, NZ):
-        class_sums = class_sums + szr[s].astype(F32)
+        first_sums = first_sums + szr[s].astype(F32)
         total = total + tzr[s]
-    mh[0] = class_sums - own_counts * (total / grand)
+    got(fxr.at[1:NX], (ffr, 1))
+    for s in range(1, NX):
+        other_sums = other_sums + fxr[s].astype(F32)
+    mean_act = total / grand
+    mh[0, :, 0:XW] = first_sums - own_counts * mean_act[:, 0:XW]
+    mh[0, :, XW:] = other_sums - own_counts * mean_act[:, XW:]
     send(mh.at[0], mh.at[1], (exs, 6), (exr, 6), other)
-    gathered(0)
 
     def twice(a, b, dims):
         high = a.astype(BF16).astype(F32)
@@ -236,26 +273,20 @@
     gy[0] = gsum.astype(BF16)
     along_y(FAR, lambda s: gy.at[0], lambda t: gy.at[t], (ggs, 0), lambda t: (ggr, 0))
 
-    got(lg.at[1:NX], (lxr, 0))
-    send(lg, lo, (exs, 2), (exr, 2), other)
-    for k in range(2):
-        lm[k * K2 : (k + 1) * K2, :] = lg[:, 4 * k : 4 * k + 4].astype(F32).reshape(K2, D).astype(BF16)
-    gathered(1)
     got(lo, (exr, 2))
     for k in range(2, 4):
         lm[k * K2 : (k + 1) * K2, :] = lo[:, 4 * k - 8 : 4 * k - 4].astype(F32).reshape(K2, D).astype(BF16)
-    for k in range(2):
-        got(cbuf.at[1, k], (fcr, k))
-
-    coords = jnp.concatenate([cbuf[0, 0], cbuf[0, 1], cbuf[1, 0], cbuf[1, 1]], axis=1)
-    for rows in (theirs, mine):
-        at = rows.start
-        corr = jnp.dot(coords[at : at + TOK], lm[:, half], preferred_element_type=F32)
-        er[rows, :] = (actv[rows, half].astype(F32) - corr).astype(BF16)
-        if at:
-            send(er.at[theirs], out.at[:, half], (exs, 3), (exr, 3), other)
-    keep = pltpu.make_async_copy(er.at[mine], out.at[:, half], loc.at[6])
-    keep.start()
+    gathered(0)
+    gathered(1)
+
+    coords = jnp.concatenate([cbuf[0, 0:TOK], cbuf[1, 0:TOK], cbuf[0, TOK:T2], cbuf[1, TOK:T2]], axis=1)
+    keeps = []
+    for q in range(2):
+        cols = pl.ds(q * H, H)
+        corr = jnp.dot(coords, lm[:, cols], preferred_element_type=F32)
+        er[:, cols] = (actv[mine, cols].astype(F32) - corr).astype(BF16)
+        keeps.append(pltpu.make_async_copy(er.at[:, cols], out.at[:, cols], loc.at[6 + q]))
+        keeps[q].start()
 
     got(gy.at[1:NY], (ggr, 0))
     for s in range(1, NY):
@@ -276,7 +307,8 @@
     for k, cols in enumerate((half, their_half)):
         scores[:, cols] += mh[k, ours, :] * scale
 
-    keep.wait()
+    for cp in keeps:
+        cp.wait()
     gone(rg.at[0, 1:NZ], (rzs, 0))
     gone(rg.at[1:NX], (rxs, 0))
     gone(lab.at[0, 0, 1:NZ], (bzs, 0))
@@ -286,20 +318,29 @@
     gone(actv.at[mine], (exs, 0))
     gone(lab.at[0], (exs, 1))
     gone(lo, (exs, 2))
-    gone(er.at[theirs], (exs, 3))
     for k in range(2):
         gone(prx.at[k, 1:NY], (pss, k))
-        gone(prx.at[k, 1:NY], (css, k))
-        gone(cbuf.at[0, k], (fcs, k))
     gone(sxr.at[1:NX], (xxs, 0))
     gone(szr.at[1:NZ], (zzs, 0))
     gone(txr.at[1:NX], (xxs, 1))
     gone(tzr.at[1:NZ], (zzs, 1))
+
+    @pl.when(near_half)
+    def _():
+        for k in range(2):
+            gone(cbuf.at[k, 0 : T2 - YB], (css, k))
+
+    @pl.when(jnp.logical_not(near_half))
+    def _():
+        for k in range(2):
+            gone(cbuf.at[k], (css, k))
+
+    gone(fzr.at[1:NZ], (ffs, 0))
+    gone(fxr.at[1:NX], (ffs, 1))
     gone(gy.at[1:NY], (ggs, 0))
     gone(labo, (exs, 5))
     gone(mh.at[0], (exs, 6))
     gone(gx.at[0, others], (exs, 7))
-    got(er.at[theirs], (exr, 3))
 
 
 def hand_out(erased, scores, cnt, erased_out, scores_out, cnt_out, erased_v, scores_v, cnt_v, sems):
@@ -347,18 +388,24 @@
             pltpu.VMEM((1, TOK), I32),
             pltpu.VMEM((2, T2, K2), BF16),
             pltpu.VMEM((2, NY, YB, K2), BF16),
-            pltpu.VMEM((2, 2, T2, K2), BF16),
+            pltpu.VMEM((2, YB, K2), BF16),
+            pltpu.VMEM((2, T2, K2), BF16),
             pltpu.VMEM((C, T2), BF16),
-            pltpu.VMEM((T2, H), BF16),
-            pltpu.VMEM((NX, 128, H), BF16),
-            pltpu.VMEM((NX, 128, H), BF16),
-            pltpu.VMEM((128, H), F32),
+            pltpu.VMEM((TOK, D), BF16),
+            pltpu.VMEM((NX, 128, XW), BF16),
+            pltpu.VMEM((NX, 128, XW), BF16),
+            pltpu.VMEM((128, XW), F32),
             pltpu.VMEM((1, H), F32),
             pltpu.VMEM((NX, 1, H), F32),
-            pltpu.VMEM((NZ, 2 * RD, H), BF16),
-            pltpu.VMEM((NZ, 2 * RD, H), BF16),
+            pltpu.VMEM((NZ, M, XW), BF16),
+            pltpu.VMEM((NZ, M, XW), BF16),
             pltpu.VMEM((1, H), F32),
             pltpu.VMEM((NZ, 1, H), F32),
+            pltpu.VMEM((NZ, NX * M, ZW), BF16),
+            pltpu.VMEM((NZ, NX * M, ZW), BF16),
+            pltpu.VMEM((NX * M, ZW), F32),
+            pltpu.VMEM((NX, M, ZW), BF16),
+            pltpu.VMEM((NX, M, ZW), BF16),
             pltpu.VMEM((2, M, H), F32),
             pltpu.VMEM((256, D), BF16),
             pltpu.VMEM((NY, M, 256), BF16),
@@ -373,7 +420,7 @@
             dma((1,)), dma((1,)),
             dma((8,)), dma((8,)),
             dma((2,)), dma((2,)),
-            dma((2,)), dma((2 * NY,)),
+            dma((2,)), dma((2,)),
             dma((2,)), dma((2,)),
             dma((2,)), dma((2,)),
             dma((2,)), dma((2,)),

time: 51.1 us -> 48.6 us (0.951)
  Pallas kernels: 49.6 us -> 47.1 us
    pallas_call x1, Pallas kernels: 47.7 us -> 45.3 us  [per_device(): pl.pallas_call(kernel, out_shape=shapes, in_specs=[hbm] * 6, out_specs=(a...]
where the time goes in v5:
time: 48.6 us; the launch traced here: 48.4 us
  Pallas kernels  47.1 us (97%)
  between operations  1.29 us (3%)
    pallas_call x1, Pallas kernels, per_device(): pl.pallas_call(kernel, out_shape=shapes, in_specs=[hbm] * 6, out_specs=(a...  45.3 us
    pallas_call x1, Pallas kernels, per_device(): pl.pallas_call(hand_out, out_shape=shapes, in_specs=[hbm] * 3, out_specs=...  1.86 us

profile of v5, /device:TPU:1, one launch (start us, length us, event | category | flops | bytes accessed | tf_op | source)
XLA Modules:
  0.0 48.4 jit_solution(8569268545592098719)
XLA Ops:
  1.3 45.3 %shard_map.85 = (bf16[256,1024]{1,0:T(8,128)(2,1)}, f32[8,1024]{1,0:T(8,128)}, s32[1,8]{1,0:T(1,128)}) custom-call(bf16[256,1024]{1,0:T(8,128)(2,1)} %acts.1, f32[1,1024]{1,0:T(1,128)} %bitcast.3, bf16[8,1024]{1,0:T(8,128)(2,1)} %left.1, bf16[8,1024]{1,0:T(8,128)(2,1)} %right.1, s32[1,256]{1,0:T(1,128)} %bitcast.4, s32[1]{0:T(128)S(6)} %copy.9.counts), custom_call_target="tpu_custom_call" | custom-call | flops 805306368 | bytes 4194304 | tf_op jit(solution)/shard_map/pallas_call | solution.py:372
  46.6 1.9 %shard_map.86 = (bf16[256,1024]{1,0:T(8,128)(2,1)}, f32[8,1024]{1,0:T(8,128)}, s32[1,8]{1,0:T(1,128)}) custom-call(bf16[256,1024]{1,0:T(8,128)(2,1)} %get-tuple-element.9.erased, f32[8,1024]{1,0:T(8,128)} %get-tuple-element.10.scores, s32[1,8]{1,0:T(1,128)} %get-tuple-element.11.cnt), custom_call_target="tpu_custom_call" | custom-call | tf_op jit(solution)/shard_map/pallas_call | solution.py:441

commit v6 on v5

--- a/solution.py
+++ b/solution.py
@@ -23,7 +23,7 @@
 M = 2 * RD
 XW, ZW = 384, 128
 YB = T2 // NY
-VLIM = 63 << 20
+VLIM = 40 << 20
 PIECES = 4
 
 
@@ -98,7 +98,7 @@
         cp.start()
 
     barrier = pltpu.get_barrier_semaphore()
-    peers = [dev(dz=ZORD[s]) for s in FAR] + [dev(dy=ZORD[s], core=k) for s in FAR for k in (c, oc)]
+    peers = [dev(dz=ZORD[s]) for s in FAR] + [dev(dy=ZORD[s]) for s in FAR]
     peers += [dev(dx=d) for d in (2, 1, 3)] + [other]
     for p in peers:
         pl.semaphore_signal(barrier, inc=1, device_id=p, device_id_type=MESH)
@@ -244,10 +244,6 @@
     own_counts = jnp.sum(hits, axis=1, keepdims=True)
     grand = jnp.sum(valid, axis=1, keepdims=True)
 
-    got(lg.at[1:NX], (lxr, 0))
-    send(lg, lo, (exs, 2), (exr, 2), other)
-    for k in range(2):
-        lm[k * K2 : (k + 1) * K2, :] = lg[:, 4 * k : 4 * k + 4].astype(F32).reshape(K2, D).astype(BF16)
     got(szr.at[1:NZ], (zzr, 0))
     got(tzr.at[1:NZ], (zzr, 1))
     first_sums, other_sums, total = mh[0, :, 0:XW], mh[0, :, XW:], tzs[...]
@@ -273,6 +269,10 @@
     gy[0] = gsum.astype(BF16)
     along_y(FAR, lambda s: gy.at[0], lambda t: gy.at[t], (ggs, 0), lambda t: (ggr, 0))
 
+    got(lg.at[1:NX], (lxr, 0))
+    send(lg, lo, (exs, 2), (exr, 2), other)
+    for k in range(2):
+        lm[k * K2 : (k + 1) * K2, :] = lg[:, 4 * k : 4 * k + 4].astype(F32).reshape(K2, D).astype(BF16)
     got(lo, (exr, 2))
     for k in range(2, 4):
         lm[k * K2 : (k + 1) * K2, :] = lo[:, 4 * k - 8 : 4 * k - 4].astype(F32).reshape(K2, D).astype(BF16)
@@ -343,19 +343,12 @@
     gone(gx.at[0, others], (exs, 7))
 
 
-def hand_out(erased, scores, cnt, erased_out, scores_out, cnt_out, erased_v, scores_v, cnt_v, sems):
-    rows = TOK // PIECES
-    parts = [pl.ds(i * rows, rows) for i in range(PIECES)]
-    trips = [(erased.at[p], erased_v.at[p], erased_out.at[p]) for p in parts]
-    trips += [(scores, scores_v, scores_out), (cnt, cnt_v, cnt_out)]
-    ins = [pltpu.make_async_copy(a, v, sems.at[0, i]) for i, (a, v, _) in enumerate(trips)]
-    outs = [pltpu.make_async_copy(v, b, sems.at[1, i]) for i, (_, v, b) in enumerate(trips)]
-    for cp in ins:
+def hand_out(erased, scores, cnt, erased_out, scores_out, cnt_out, sems):
+    pairs = ((erased, erased_out), (scores, scores_out), (cnt, cnt_out))
+    copies = [pltpu.make_async_copy(a, b, sems.at[i]) for i, (a, b) in enumerate(pairs)]
+    for cp in copies:
         cp.start()
-    for load, store in zip(ins, outs):
-        load.wait()
-        store.start()
-    for cp in outs:
+    for cp in copies:
         cp.wait()
 
 
@@ -371,9 +364,8 @@
     )
     results = pl.pallas_call(
         kernel,
-        out_shape=shapes,
+        out_shape=tuple(pltpu.VMEM(v.shape, v.dtype) for v in shapes),
         in_specs=[hbm] * 6,
-        out_specs=(anywhere, vm, vm),
         scratch_shapes=[
             pltpu.VMEM((1, D), F32),
             pltpu.VMEM((1, TOK), I32),
@@ -431,21 +423,25 @@
         ),
         cost_estimate=pl.CostEstimate(flops=6 * 256 * 1024 * 512, bytes_accessed=4 << 20, transcendentals=0),
     )(
-        acts,
-        mean_vec.reshape(1, D),
-        left_factor,
-        right_factor,
-        labels.reshape(1, TOK),
+        *(
+            pltpu.with_memory_space_constraint(v, pltpu.HBM)
+            for v in (
+                acts,
+                mean_vec.reshape(1, D),
+                left_factor,
+                right_factor,
+                labels.reshape(1, TOK),
+            )
+        ),
         counts,
     )
     erased, scores, cnt = pl.pallas_call(
         hand_out,
         out_shape=shapes,
-        in_specs=[hbm] * 3,
+        in_specs=[vm] * 3,
         out_specs=(hbm,) * 3,
-        scratch_shapes=[pltpu.VMEM(v.shape, v.dtype) for v in shapes] + [dma((2, PIECES + 2))],
-        compiler_params=pltpu.CompilerParams(vmem_limit_bytes=VLIM),
-    )(*results)
+        scratch_shapes=[dma((3,))],
+    )(*(pltpu.with_memory_space_constraint(v, pltpu.VMEM) for v in results))
     return erased, scores, cnt.reshape(RD)
 
 

time: 48.6 us -> 46.3 us (0.953)
  Pallas kernels: 47.1 us -> 44.9 us
    pallas_call x2, Pallas kernels: 47.1 us -> 44.9 us  [the longest x1 44 us: per_device(): pl.pallas_call(kernel, out_shape=tuple((pltpu.VMEM(v.shape, v.dtype) for...]
where the time goes in v6:
time: 46.3 us; the launch traced here: 46.1 us
  Pallas kernels  44.9 us (97%)
  between operations  1.29 us (3%)
    pallas_call x1, Pallas kernels, per_device(): pl.pallas_call(kernel, out_shape=tuple((pltpu.VMEM(v.shape, v.dtype) for...  44 us

profile of v6, /device:TPU:1, one launch (start us, length us, event | category | flops | bytes accessed | tf_op | source)
XLA Modules:
  0.0 46.1 jit_solution(11366646322673323063)
XLA Ops:
  1.3 44.0 %shard_map.85 = (bf16[256,1024]{1,0:T(8,128)(2,1)S(1)}, f32[8,1024]{1,0:T(8,128)S(1)}, s32[1,8]{1,0:T(1,128)S(1)}) custom-call(bf16[256,1024]{1,0:T(8,128)(2,1)} %acts.1, f32[1,1024]{1,0:T(1,128)} %bitcast.3, bf16[8,1024]{1,0:T(8,128)(2,1)} %left.1, bf16[8,1024]{1,0:T(8,128)(2,1)} %right.1, s32[1,256]{1,0:T(1,128)} %bitcast.4, s32[1]{0:T(128)S(6)} %copy.9.counts), custom_call_target="tpu_custom_call" | custom-call | flops 805306368 | bytes 4194304 | tf_op jit(solution)/shard_map/pallas_call | solution.py:365
  45.3 0.8 %shard_map.86 = (bf16[256,1024]{1,0:T(8,128)(2,1)}, f32[8,1024]{1,0:T(8,128)}, s32[1,8]{1,0:T(1,128)}) custom-call(bf16[256,1024]{1,0:T(8,128)(2,1)S(1)} %get-tuple-element.9.erased, f32[8,1024]{1,0:T(8,128)S(1)} %get-tuple-element.10.scores, s32[1,8]{1,0:T(1,128)S(1)} %get-tuple-element.11.cnt), custom_call_target="tpu_custom_call" | custom-call | tf_op jit(solution)/shard_map/pallas_call | solution.py:438

commit v7 on v6

--- a/solution.py
+++ b/solution.py
@@ -133,9 +133,9 @@
             owner = lax.rem(z + ZORD[zs], NZ) * NX + lax.rem(x + XORD[xs], NX)
             at = (xs * NZ + zs) * 2 * RD
             oh[at : at + 2 * RD, :] = (owner * (2 * RD) + r == tokens).astype(F32).astype(BF16)
+    own_sums = jnp.dot(oh[:, 0:TOK], actv[mine, half], preferred_element_type=F32)
     got(actv.at[theirs], (exr, 0))
-    cen[theirs, :] = (actv[theirs, :].astype(F32) - meanv[...]).astype(BF16)
-    sums = jnp.dot(oh[...], actv[:, half], preferred_element_type=F32)
+    sums = own_sums + jnp.dot(oh[:, TOK:T2], actv[theirs, half], preferred_element_type=F32)
     for zs in range(NZ):
         for xs in range(NX):
             at = (xs * NZ + zs) * M
@@ -153,6 +153,7 @@
     along_x(lambda s: txs, lambda t: txr.at[t], (xxs, 1), lambda t: (xxr, 1))
     right_x(2)
     right_x(3)
+    cen[theirs, :] = (actv[theirs, :].astype(F32) - meanv[...]).astype(BF16)
     along_z(NEAR, lambda s: lab.at[0, 0, 0], lambda t: lab.at[0, 0, t], (bzs, 0), lambda t: (bzr, 0))
 
     def block(s):

time: 46.3 us -> 46.4 us (level)
  no operation moved by 1% of the time
where the time goes in v7:
time: 46.4 us; the launch traced here: 46.1 us
  Pallas kernels  44.9 us (97%)
  between operations  1.29 us (3%)
    pallas_call x1, Pallas kernels, per_device(): pl.pallas_call(kernel, out_shape=tuple((pltpu.VMEM(v.shape, v.dtype) for...  44 us

profile of v7, /device:TPU:1, one launch (start us, length us, event | category | flops | bytes accessed | tf_op | source)
XLA Modules:
  0.0 46.1 jit_solution(468608629216719805)
XLA Ops:
  1.3 44.0 %shard_map.85 = (bf16[256,1024]{1,0:T(8,128)(2,1)S(1)}, f32[8,1024]{1,0:T(8,128)S(1)}, s32[1,8]{1,0:T(1,128)S(1)}) custom-call(bf16[256,1024]{1,0:T(8,128)(2,1)} %acts.1, f32[1,1024]{1,0:T(1,128)} %bitcast.3, bf16[8,1024]{1,0:T(8,128)(2,1)} %left.1, bf16[8,1024]{1,0:T(8,128)(2,1)} %right.1, s32[1,256]{1,0:T(1,128)} %bitcast.4, s32[1]{0:T(128)S(6)} %copy.9.counts), custom_call_target="tpu_custom_call" | custom-call | flops 805306368 | bytes 4194304 | tf_op jit(solution)/shard_map/pallas_call | solution.py:366
  45.3 0.8 %shard_map.86 = (bf16[256,1024]{1,0:T(8,128)(2,1)}, f32[8,1024]{1,0:T(8,128)}, s32[1,8]{1,0:T(1,128)}) custom-call(bf16[256,1024]{1,0:T(8,128)(2,1)S(1)} %get-tuple-element.9.erased, f32[8,1024]{1,0:T(8,128)S(1)} %get-tuple-element.10.scores, s32[1,8]{1,0:T(1,128)S(1)} %get-tuple-element.11.cnt), custom_call_target="tpu_custom_call" | custom-call | tf_op jit(solution)/shard_map/pallas_call | solution.py:439
